TPU v7x, 32 devices: a whole 2x2x4 slice. The times are simulated.
32 devices in a mesh: group: 2 (over y), inst: 16 (over z, x, core).
Axes of the slice: x: 2, y: 2, z: 4, core: 2. Of those that a mesh axis runs over, the one named last changes fastest.
Arguments:
- kv_pool: bfloat16 [384, 128, 2048], P(('group', 'inst')), parts along dimension 0, as said below
- page_table: int32 [128, 3], P(('group', 'inst')), parts along dimension 0, may hold values from 0 to 11, as said below
- lengths: int32 [128], P(('group', 'inst')), parts along dimension 0, may hold values from 1 to 384, as said below
- query: bfloat16 [2, 128, 8192], P(None, ('group', 'inst')), parts along dimension 1, as said below
- new_kv: bfloat16 [2, 128, 2048], P(None, ('group', 'inst')), parts along dimension 1, may hold values from -6 to 6
- moves: int32 [128], P(('group', 'inst')), parts along dimension 0, may hold values from 0 to 3, as said below
Outputs:
- attended: bfloat16 [2, 128, 8192], P(None, ('group', 'inst')), parts along dimension 1
- guest_attended: bfloat16 [96, 8192], P(('group', 'inst')), parts along dimension 0
- moved_pages: bfloat16 [288, 128, 2048], P(('group', 'inst')), parts along dimension 0
There are 2 independent parts, one for each index of `group`. A program takes and returns all parts, laid end to end along the dimension named above; each array names one. Nothing has to cross between parts.
Inputs may be any that keep to these rules, and one draw needn't show every extreme that they name: `page_table`: within one instance, the 4 sessions' page-table rows together name each of its 12 slots once. `lengths`: some session holds the full 3 pages. `moves`: among the sessions of one instance each distance 1 to 3 occurs exactly once; the others are 0. `query`: query entries are of order one or up to some tens. `kv_pool`: cached entries are of order one.
All inputs are finite; a program needn't handle non-finite values.
Results may differ from a plain program's by a relative error of at most 0.0051.
Values may be sent and summed in bfloat16 or wider, within the bound.
No kernel may reach another device: no remote copies, remote signals or barrier semaphores. Data moves between devices by JAX's collectives and lax.ppermute only.
A program may use at most 64 MiB of HBM per device.

v0:
```python
import jax
import jax.numpy as jnp
from jax import lax
from jax.sharding import PartitionSpec as P

HQ = 64
KVH = 8
HD = 128
REACH = 3
GRP = 8


def shifted(value, axis, steps):
    count = lax.axis_size(axis)
    pairs = [(source, (source + steps) % count) for source in range(count)]
    return lax.ppermute(value, axis, pairs)


def attend_one(cached, visible, query_row, fresh_row):
    flat_rows = cached.reshape(-1, 2, KVH, HD)
    key_rows = flat_rows[:, 0]
    value_rows = flat_rows[:, 1]
    query_heads = query_row.reshape(KVH, GRP, HD)
    fresh = fresh_row.reshape(2, KVH, HD)
    scale = 1.0 / jnp.sqrt(jnp.float32(HD))
    scores = (
        jnp.einsum("kgd,tkd->kgt", query_heads, key_rows, preferred_element_type=jnp.float32)
        * scale
    )
    own_score = (
        jnp.einsum("kgd,kd->kg", query_heads, fresh[0], preferred_element_type=jnp.float32) * scale
    )
    scores = jnp.where(visible[None, None, :], scores, jnp.float32(-1e30))
    highest = jnp.maximum(jnp.max(scores, axis=-1), own_score)
    expo = jnp.exp(scores - highest[..., None])
    own_expo = jnp.exp(own_score - highest)
    denominator = jnp.sum(expo, axis=-1) + own_expo
    weights = (expo / denominator[..., None]).astype(jnp.bfloat16)
    own_weight = (own_expo / denominator).astype(jnp.bfloat16)
    result = jnp.einsum("kgt,tkd->kgd", weights, value_rows, preferred_element_type=jnp.float32)
    result = (
        result
        + own_weight.astype(jnp.float32)[..., None] * fresh[1].astype(jnp.float32)[:, None, :]
    )
    return result.reshape(HQ * HD).astype(jnp.bfloat16)


def body(kv_pool, page_table, lengths, query, new_kv, moves):
    sessions_here = page_table.shape[0]
    page_rows = kv_pool.shape[1]
    positions = jnp.arange(page_table.shape[1] * page_rows, dtype=jnp.int32)
    visible = positions[None, :] < lengths[:, None]
    cached = kv_pool[page_table]
    run_all = jax.vmap(attend_one)
    earlier = run_all(cached, visible, query[0], new_kv[0])
    ordering = jnp.argsort(moves, stable=True)
    staying = sessions_here - REACH
    movers = ordering[staying:]
    out_pages = cached[movers]
    out_visible = visible[movers].astype(jnp.bfloat16)
    out_query = query[1][movers]
    out_fresh = new_kv[1][movers]
    arrived = []
    for offset in range(1, REACH + 1):
        arrived.append(
            shifted(
                (
                    out_pages[offset - 1],
                    out_visible[offset - 1],
                    out_query[offset - 1],
                    out_fresh[offset - 1],
                ),
                "inst",
                offset,
            )
        )
    recv_pages = jnp.stack([item[0] for item in arrived])
    moved_pages = recv_pages.reshape(-1, page_rows, recv_pages.shape[-1])
    stay_index = ordering[:staying]
    stay_out = run_all(
        cached[stay_index], visible[stay_index], query[1][stay_index], new_kv[1][stay_index]
    )
    second = jnp.zeros_like(earlier).at[stay_index].set(stay_out)
    recv_visible = jnp.stack([item[1] for item in arrived]) > 0
    recv_query = jnp.stack([item[2] for item in arrived])
    recv_fresh = jnp.stack([item[3] for item in arrived])
    guest_attended = run_all(recv_pages, recv_visible, recv_query, recv_fresh)
    return (jnp.stack([earlier, second]), guest_attended, moved_pages)


def solution(mesh):
    return jax.shard_map(
        body,
        mesh=mesh,
        in_specs=(
            P(("group", "inst"), None, None),
            P(("group", "inst"), None),
            P(("group", "inst")),
            P(None, ("group", "inst"), None),
            P(None, ("group", "inst"), None),
            P(("group", "inst")),
        ),
        out_specs=(
            P(None, ("group", "inst"), None),
            P(("group", "inst"), None),
            P(("group", "inst"), None, None),
        ),
        check_vma=False,
    )
```

profile of v0, /device:TPU:0, one launch (start us, length us, event | category | flops | bytes accessed | tf_op | source)
XLA Modules:
  0.0 139.9 jit_solution(11916732679369429260)
XLA Ops:
  0.6 1.4 sort.17
  2.1 0.7 compare_select_fusion
  2.9 7.0 %gather_fusion = bf16[12,128,2048]{2,1,0:T(8,128)(2,1)} fusion(bf16[12,128,2048]{2,1,0:T(8,128)(2,1)} %param.8, s32[1024]{0:T(1024)S(1)} %get-tuple-element.102), kind=kCustom, calls=%fused_computation | custom fusion | bytes 12582960 | tf_op jit(solution)/shard_map/gather | solution.py:53
  9.9 6.0 %gather_fusion.3 = bf16[3,3,128,2048]{3,2,1,0:T(8,128)(2,1)} fusion(bf16[4,3,128,2048]{3,2,1,0:T(8,128)(2,1)} %bitcast.155, s32[1024]{0:T(1024)S(1)} %get-tuple-element.101), kind=kCustom, calls=%fused_computation.3 | custom fusion | bytes 9437196 | tf_op jit(solution)/shard_map/gather | solution.py:59
  15.8 4.7 %slice_bitcast_fusion.4 = (bf16[3,128,2048]{2,1,0:T(8,128)(2,1)}, bf16[3,128,2048]{2,1,0:T(8,128)(2,1)}, bf16[3,128,2048]{2,1,0:T(8,128)(2,1)}) fusion(bf16[3,3,128,2048]{3,2,1,0:T(8,128)(2,1)} %gather_fusion.3), kind=kLoop, calls=%fused_computation.14 | loop fusion | bytes 9437184 | tf_op jit(solution)/shard_map/squeeze | solution.py:68
  20.5 0.5 collective-permute-start.6
  21.0 2.5 %collective-permute-start.7 = (bf16[3,128,2048]{2,1,0:T(8,128)(2,1)}, bf16[3,128,2048]{2,1,0:T(8,128)(2,1)S(1)}, u32[]{:S(2)}, u32[]{:S(2)}) collective-permute-start(bf16[3,128,2048]{2,1,0:T(8,128)(2,1)} %get-tuple-element.73), channel_id=1, source_target_pairs={{0,2},{1,3},{2,4},{3,5},{4,6},{5,7},{6,8},{7,9},{8,10},{9,11},{10,... | collective-permute-start | bytes 4718600 | tf_op jit(solution)/shard_map/ppermute | solution.py:16
  23.5 2.5 %collective-permute-start.8 = (bf16[3,128,2048]{2,1,0:T(8,128)(2,1)}, bf16[3,128,2048]{2,1,0:T(8,128)(2,1)}, u32[]{:S(2)}, u32[]{:S(2)}) collective-permute-start(bf16[3,128,2048]{2,1,0:T(8,128)(2,1)} %get-tuple-element.72), channel_id=1, source_target_pairs={{0,3},{1,4},{2,5},{3,6},{4,7},{5,8},{6,9},{7,10},{8,11},{9,12},{10... | collective-permute-start | bytes 4718600 | tf_op jit(solution)/shard_map/ppermute | solution.py:16
  26.0 0.6 gather_fusion.1
  26.6 0.4 collective-permute-start.2
  27.1 1.5 %collective-permute-start.1 = (bf16[384]{0:T(512)(128)(2,1)S(1)}, bf16[384]{0:T(512)(128)(2,1)S(1)}, u32[]{:S(2)}, u32[]{:S(2)}) collective-permute-start(bf16[384]{0:T(512)(128)(2,1)S(1)} %get-tuple-element.69), channel_id=1, source_target_pairs={{0,2},{1,3},{2,4},{3,5},{4,6},{5,7},{6,8},{7,9},{8,10},{9,11},{10,... | collective-permute-start | bytes 2312 | tf_op jit(solution)/shard_map/ppermute | solution.py:16
  28.7 1.5 %constant_dynamic-slice_fusion = bf16[1,3,128,2048]{3,2,1,0:T(8,128)(2,1)S(1)} fusion(bf16[4,3,128,2048]{3,2,1,0:T(8,128)(2,1)} %bitcast.156, s32[]{:T(128)} %bitcast.8), kind=kLoop, calls=%fused_computation.116 | loop fusion | bytes 3145732 | tf_op jit(solution)/shard_map/gather | solution.py:81
  30.3 0.4 copy.32
  30.8 0.3 copy-done
  31.5 0.5 fusion.53
  32.2 0.7 and_reduce_fusion
  32.9 0.9 fusion.15
  33.9 5.1 %copy.29 = bf16[192,8,16,128]{3,2,1,0:T(8,128)(2,1)S(1)} copy(bf16[192,8,16,128]{3,1,2,0:T(8,128)(2,1)} %bitcast.157) | data formatting | bytes 12582912
  39.0 1.1 fusion.51
  40.2 1.3 fusion.54
  41.9 0.7 fusion.9
  42.7 0.3 scatter.4
  43.0 0.7 pad_maximum_fusion.1
  43.8 0.6 gather_fusion.4
  44.4 0.6 gather_fusion.2
  45.0 46.7 %collective-permute-done.2 = bf16[384]{0:T(512)(128)(2,1)S(1)} collective-permute-done((bf16[384]{0:T(512)(128)(2,1)S(1)}, bf16[384]{0:T(512)(128)(2,1)S(1)}, u32[]{:S(2)}, u32[]{:S(2)}) %collective-permute-start.2) | collective-permute-done | bytes 800 | tf_op jit(solution)/shard_map/ppermute | solution.py:16
  91.7 3.9 %collective-permute-start = (bf16[384]{0:T(512)(128)(2,1)S(1)}, bf16[384]{0:T(512)(128)(2,1)S(1)}, u32[]{:S(2)}, u32[]{:S(2)}) collective-permute-start(bf16[384]{0:T(512)(128)(2,1)S(1)} %get-tuple-element.67), channel_id=1, source_target_pairs={{0,1},{1,2},{2,3},{3,4},{4,5},{5,6},{6,7},{7,8},{8,9},{9,10},{10,1... | collective-permute-start | bytes 2312 | tf_op jit(solution)/shard_map/ppermute | solution.py:16
  95.7 14.1 %collective-permute-start.11 = (bf16[2048]{0:T(1024)(128)(2,1)S(1)}, bf16[2048]{0:T(1024)(128)(2,1)S(1)}, u32[]{:S(2)}, u32[]{:S(2)}) collective-permute-start(bf16[2048]{0:T(1024)(128)(2,1)S(1)} %get-tuple-element.66), channel_id=1, source_target_pairs={{0,3},{1,4},{2,5},{3,6},{4,7},{5,8},{6,9},{7,10},{8,11},{9,12},{10... | collective-permute-start | bytes 12296 | tf_op jit(solution)/shard_map/ppermute | solution.py:16
  109.8 0.3 slice_reduce_fusion.2
  110.1 2.2 %collective-permute-done = bf16[384]{0:T(512)(128)(2,1)S(1)} collective-permute-done((bf16[384]{0:T(512)(128)(2,1)S(1)}, bf16[384]{0:T(512)(128)(2,1)S(1)}, u32[]{:S(2)}, u32[]{:S(2)}) %collective-permute-start) | collective-permute-done | bytes 800 | tf_op jit(solution)/shard_map/ppermute | solution.py:16
  112.3 3.0 %collective-permute-start.10 = (bf16[2048]{0:T(1024)(128)(2,1)S(1)}, bf16[2048]{0:T(1024)(128)(2,1)S(1)}, u32[]{:S(2)}, u32[]{:S(2)}) collective-permute-start(bf16[2048]{0:T(1024)(128)(2,1)S(1)} %get-tuple-element.65), channel_id=1, source_target_pairs={{0,2},{1,3},{2,4},{3,5},{4,6},{5,7},{6,8},{7,9},{8,10},{9,11},{10,... | collective-permute-start | bytes 12296 | tf_op jit(solution)/shard_map/ppermute | solution.py:16
  115.6 2.6 %collective-permute-start.9 = (bf16[2048]{0:T(1024)(128)(2,1)S(1)}, bf16[2048]{0:T(1024)(128)(2,1)S(1)}, u32[]{:S(2)}, u32[]{:S(2)}) collective-permute-start(bf16[2048]{0:T(1024)(128)(2,1)S(1)} %get-tuple-element.64), channel_id=1, source_target_pairs={{0,1},{1,2},{2,3},{3,4},{4,5},{5,6},{6,7},{7,8},{8,9},{9,10},{10,1... | collective-permute-start | bytes 12296 | tf_op jit(solution)/shard_map/ppermute | solution.py:16
  118.2 0.5 collective-permute-done.10
  118.8 2.6 %collective-permute-done.9 = bf16[2048]{0:T(1024)(128)(2,1)S(1)} collective-permute-done((bf16[2048]{0:T(1024)(128)(2,1)S(1)}, bf16[2048]{0:T(1024)(128)(2,1)S(1)}, u32[]{:S(2)}, u32[]{:S(2)}) %collective-permute-start.9) | collective-permute-done | bytes 4128 | tf_op jit(solution)/shard_map/ppermute | solution.py:16
  121.4 2.3 %collective-permute-done.5 = bf16[8192]{0:T(1024)(128)(2,1)S(1)} collective-permute-done((bf16[8192]{0:T(1024)(128)(2,1)S(1)}, bf16[8192]{0:T(1024)(128)(2,1)S(1)}, u32[]{:S(2)}, u32[]{:S(2)}) %collective-permute-start.5) | collective-permute-done | bytes 16416 | tf_op jit(solution)/shard_map/ppermute | solution.py:16
  123.7 0.5 collective-permute-start.3
  124.2 3.6 %collective-permute-done.4 = bf16[8192]{0:T(1024)(128)(2,1)S(1)} collective-permute-done((bf16[8192]{0:T(1024)(128)(2,1)S(1)}, bf16[8192]{0:T(1024)(128)(2,1)S(1)}, u32[]{:S(2)}, u32[]{:S(2)}) %collective-permute-start.4) | collective-permute-done | bytes 16416 | tf_op jit(solution)/shard_map/ppermute | solution.py:16
  127.8 1.8 %collective-permute-done.3 = bf16[8192]{0:T(1024)(128)(2,1)S(1)} collective-permute-done((bf16[8192]{0:T(1024)(128)(2,1)S(1)}, bf16[8192]{0:T(1024)(128)(2,1)S(1)}, u32[]{:S(2)}, u32[]{:S(2)}) %collective-permute-start.3) | collective-permute-done | bytes 16416 | tf_op jit(solution)/shard_map/ppermute | solution.py:16
  129.7 0.4 copy.33
  130.2 0.4 copy.34
  130.6 0.4 copy_dynamic-update-slice_fusion.2
  131.0 1.8 %copy.35 = bf16[48,8,16,128]{3,2,1,0:T(8,128)(2,1)S(1)} copy(bf16[48,8,16,128]{3,1,2,0:T(8,128)(2,1)} %bitcast.74) | data formatting | bytes 3145728
  132.8 0.5 copy_dynamic-update-slice_fusion.1
  133.3 0.5 copy_dynamic-update-slice_fusion
  133.8 1.0 select_reduce_fusion
  135.1 0.6 fusion.13
  135.7 0.7 copy.80
  136.4 3.6 %pad_maximum_fusion = bf16[3,3,128,2048]{3,2,1,0:T(8,128)(2,1)} fusion(bf16[1,3,128,2048]{3,2,1,0:T(8,128)(2,1)} %bitcast.37, bf16[1,3,128,2048]{3,2,1,0:T(8,128)(2,1)S(1)} %bitcast.162, bf16[1,3,128,2048]{3,2,1,0:T(8,128)(2,1)S(1)} %bitcast.160), kind=kLoop, calls=%fused_computation.5 | loop fusion | flops 4718592 | bytes 9437184 | tf_op jit(solution)/shard_map/stack | solution.py:77
  (52 shorter events, 2.4 us)
Async XLA Ops:
  15.8 10.1 %copy-start.2 = (s32[4]{0:T(128)S(1)}, s32[4]{0:T(128)}, u32[]{:S(2)}) copy-start(s32[4]{0:T(128)} %param.10) | copy-start | bytes 52
  20.5 109.2 %collective-permute-start.6 = (bf16[3,128,2048]{2,1,0:T(8,128)(2,1)}, bf16[3,128,2048]{2,1,0:T(8,128)(2,1)S(1)}, u32[]{:S(2)}, u32[]{:S(2)}) collective-permute-start(bf16[3,128,2048]{2,1,0:T(8,128)(2,1)} %get-tuple-element.74), channel_id=1, source_target_pairs={{0,1},{1,2},{2,3},{3,4},{4,5},{5,6},{6,7},{7,8},{8,9},{9,10},{10,1... | collective-permute-start | bytes 4718600 | tf_op jit(solution)/shard_map/ppermute | solution.py:16
  21.0 109.2 %collective-permute-start.7 = (bf16[3,128,2048]{2,1,0:T(8,128)(2,1)}, bf16[3,128,2048]{2,1,0:T(8,128)(2,1)S(1)}, u32[]{:S(2)}, u32[]{:S(2)}) collective-permute-start(bf16[3,128,2048]{2,1,0:T(8,128)(2,1)} %get-tuple-element.73), channel_id=1, source_target_pairs={{0,2},{1,3},{2,4},{3,5},{4,6},{5,7},{6,8},{7,9},{8,10},{9,11},{10,... | collective-permute-start | bytes 4718600 | tf_op jit(solution)/shard_map/ppermute | solution.py:16
  23.5 107.5 %collective-permute-start.8 = (bf16[3,128,2048]{2,1,0:T(8,128)(2,1)}, bf16[3,128,2048]{2,1,0:T(8,128)(2,1)}, u32[]{:S(2)}, u32[]{:S(2)}) collective-permute-start(bf16[3,128,2048]{2,1,0:T(8,128)(2,1)} %get-tuple-element.72), channel_id=1, source_target_pairs={{0,3},{1,4},{2,5},{3,6},{4,7},{5,8},{6,9},{7,10},{8,11},{9,12},{10... | collective-permute-start | bytes 4718600 | tf_op jit(solution)/shard_map/ppermute | solution.py:16
  26.6 65.0 %collective-permute-start.2 = (bf16[384]{0:T(512)(128)(2,1)S(1)}, bf16[384]{0:T(512)(128)(2,1)S(1)}, u32[]{:S(2)}, u32[]{:S(2)}) collective-permute-start(bf16[384]{0:T(512)(128)(2,1)S(1)} %get-tuple-element.68), channel_id=1, source_target_pairs={{0,3},{1,4},{2,5},{3,6},{4,7},{5,8},{6,9},{7,10},{8,11},{9,12},{10... | collective-permute-start | bytes 2312 | tf_op jit(solution)/shard_map/ppermute | solution.py:16
  27.1 68.6 %collective-permute-start.1 = (bf16[384]{0:T(512)(128)(2,1)S(1)}, bf16[384]{0:T(512)(128)(2,1)S(1)}, u32[]{:S(2)}, u32[]{:S(2)}) collective-permute-start(bf16[384]{0:T(512)(128)(2,1)S(1)} %get-tuple-element.69), channel_id=1, source_target_pairs={{0,2},{1,3},{2,4},{3,5},{4,6},{5,7},{6,8},{7,9},{8,10},{9,11},{10,... | collective-permute-start | bytes 2312 | tf_op jit(solution)/shard_map/ppermute | solution.py:16
  30.2 0.9 copy-start
  30.2 1.1 copy-start.1
  30.7 1.5 %copy-start.3 = (s32[2]{0:T(128)S(1)}, s32[2]{0:T(128)}, u32[]{:S(2)}) copy-start(s32[2]{0:T(128)} %constant.46.clone.1) | copy-start | bytes 28
  91.7 20.6 %collective-permute-start = (bf16[384]{0:T(512)(128)(2,1)S(1)}, bf16[384]{0:T(512)(128)(2,1)S(1)}, u32[]{:S(2)}, u32[]{:S(2)}) collective-permute-start(bf16[384]{0:T(512)(128)(2,1)S(1)} %get-tuple-element.67), channel_id=1, source_target_pairs={{0,1},{1,2},{2,3},{3,4},{4,5},{5,6},{6,7},{7,8},{8,9},{9,10},{10,1... | collective-permute-start | bytes 2312 | tf_op jit(solution)/shard_map/ppermute | solution.py:16
  95.7 19.9 %collective-permute-start.11 = (bf16[2048]{0:T(1024)(128)(2,1)S(1)}, bf16[2048]{0:T(1024)(128)(2,1)S(1)}, u32[]{:S(2)}, u32[]{:S(2)}) collective-permute-start(bf16[2048]{0:T(1024)(128)(2,1)S(1)} %get-tuple-element.66), channel_id=1, source_target_pairs={{0,3},{1,4},{2,5},{3,6},{4,7},{5,8},{6,9},{7,10},{8,11},{9,12},{10... | collective-permute-start | bytes 12296 | tf_op jit(solution)/shard_map/ppermute | solution.py:16
  112.3 6.4 %collective-permute-start.10 = (bf16[2048]{0:T(1024)(128)(2,1)S(1)}, bf16[2048]{0:T(1024)(128)(2,1)S(1)}, u32[]{:S(2)}, u32[]{:S(2)}) collective-permute-start(bf16[2048]{0:T(1024)(128)(2,1)S(1)} %get-tuple-element.65), channel_id=1, source_target_pairs={{0,2},{1,3},{2,4},{3,5},{4,6},{5,7},{6,8},{7,9},{8,10},{9,11},{10,... | collective-permute-start | bytes 12296 | tf_op jit(solution)/shard_map/ppermute | solution.py:16
  115.6 5.7 %collective-permute-start.9 = (bf16[2048]{0:T(1024)(128)(2,1)S(1)}, bf16[2048]{0:T(1024)(128)(2,1)S(1)}, u32[]{:S(2)}, u32[]{:S(2)}) collective-permute-start(bf16[2048]{0:T(1024)(128)(2,1)S(1)} %get-tuple-element.64), channel_id=1, source_target_pairs={{0,1},{1,2},{2,3},{3,4},{4,5},{5,6},{6,7},{7,8},{8,9},{9,10},{10,1... | collective-permute-start | bytes 12296 | tf_op jit(solution)/shard_map/ppermute | solution.py:16
  118.8 5.0 %collective-permute-start.5 = (bf16[8192]{0:T(1024)(128)(2,1)S(1)}, bf16[8192]{0:T(1024)(128)(2,1)S(1)}, u32[]{:S(2)}, u32[]{:S(2)}) collective-permute-start(bf16[8192]{0:T(1024)(128)(2,1)S(1)} %get-tuple-element.63), channel_id=1, source_target_pairs={{0,3},{1,4},{2,5},{3,6},{4,7},{5,8},{6,9},{7,10},{8,11},{9,12},{10... | collective-permute-start | bytes 49160 | tf_op jit(solution)/shard_map/ppermute | solution.py:16
  121.4 6.4 %collective-permute-start.4 = (bf16[8192]{0:T(1024)(128)(2,1)S(1)}, bf16[8192]{0:T(1024)(128)(2,1)S(1)}, u32[]{:S(2)}, u32[]{:S(2)}) collective-permute-start(bf16[8192]{0:T(1024)(128)(2,1)S(1)} %get-tuple-element.62), channel_id=1, source_target_pairs={{0,2},{1,3},{2,4},{3,5},{4,6},{5,7},{6,8},{7,9},{8,10},{9,11},{10,... | collective-permute-start | bytes 49160 | tf_op jit(solution)/shard_map/ppermute | solution.py:16
  123.7 5.9 %collective-permute-start.3 = (bf16[8192]{0:T(1024)(128)(2,1)S(1)}, bf16[8192]{0:T(1024)(128)(2,1)S(1)}, u32[]{:S(2)}, u32[]{:S(2)}) collective-permute-start(bf16[8192]{0:T(1024)(128)(2,1)S(1)} %get-tuple-element.61), channel_id=1, source_target_pairs={{0,1},{1,2},{2,3},{3,4},{4,5},{5,6},{6,7},{7,8},{8,9},{9,10},{10,1... | collective-permute-start | bytes 49160 | tf_op jit(solution)/shard_map/ppermute | solution.py:16
where the time goes:
time: 140 us
  waiting for transfers between devices  60.1 us (43%)
  local copies, waits for them, and re-layouts  33.9 us (24%)
  starting transfers between devices  31.5 us (22%)
  other arithmetic  8 us (6%)
  matrix products  5.36 us (4%)
    ppermute x12, waiting for transfers between devices, shifted(): return lax.ppermute(value, axis, pairs)  60.1 us
    ppermute x12, starting transfers between devices, shifted(): return lax.ppermute(value, axis, pairs)  31.5 us
    unnamed x17, local copies, waits for them, and re-layouts  10.1 us
    gather x1, local copies, waits for them, and re-layouts, body(): cached = kv_pool[page_table]  6.99 us
    gather x1, local copies, waits for them, and re-layouts, body(): out_pages = cached[movers]  5.97 us
    squeeze x1, local copies, waits for them, and re-layouts, body(): out_pages[offset - 1]  4.69 us
    another operation x1, other arithmetic, body(): recv_pages = jnp.stack([item[0] for item in arrived])  3.57 us
  transfers between devices with their start and end apart: 12, of which 9 were waited for; matrix products, arithmetic and copies ran while one was open for 13% of the time, Pallas kernels for 0%

commit v1 on v0

v1 whole, which is shorter than its diff:
```python
import functools

import jax
import jax.numpy as jnp
from jax import lax
from jax.experimental import pallas as pl
from jax.experimental.pallas import tpu as pltpu
from jax.sharding import PartitionSpec as P

HQ = 64
KVH = 8
HD = 128
REACH = 3
GRP = 8
STEPS = 2


def send(value, pairs):
    return lax.ppermute(value, "inst", pairs)


def shift_pairs(count, steps):
    return [(source, (source + steps) % count) for source in range(count)]


def relay_pairs(count):
    first = [(i, i - 3 if i % 4 == 3 else i + 1) for i in range(count)]
    second = [(i, (i + 4) % count if i % 4 == 0 else i) for i in range(count)]
    return first, second


def pack_kernel(moves_ref, table_ref, pool_ref, *refs):
    outs, sems = refs[:REACH], refs[REACH]
    copies = []
    for offset in range(1, REACH + 1):
        mover = jnp.int32(0)
        for session in range(1, table_ref.shape[0]):
            mover = jnp.where(moves_ref[session] == offset, jnp.int32(session), mover)
        for page in range(table_ref.shape[1]):
            copies.append(
                pltpu.make_async_copy(
                    pool_ref.at[table_ref[mover, page]],
                    outs[offset - 1].at[page],
                    sems.at[offset - 1, page],
                )
            )
            copies[-1].start()
    for copy in copies:
        copy.wait()


def pack(moves, page_table, kv_pool):
    pages = page_table.shape[1]
    piece = jax.ShapeDtypeStruct((pages,) + kv_pool.shape[1:], kv_pool.dtype)
    return pl.pallas_call(
        pack_kernel,
        out_shape=(piece,) * REACH,
        in_specs=[
            pl.BlockSpec(memory_space=pltpu.SMEM),
            pl.BlockSpec(memory_space=pltpu.SMEM),
            pl.BlockSpec(memory_space=pl.ANY),
        ],
        out_specs=(pl.BlockSpec(memory_space=pl.ANY),) * REACH,
        scratch_shapes=[pltpu.SemaphoreType.DMA((REACH, pages))],
        name="pack",
    )(moves, page_table, kv_pool)


def place_kernel(row, piece_ref, *refs):
    out_ref, sem = refs[-2], refs[-1]
    copy = pltpu.make_async_copy(piece_ref, out_ref.at[pl.ds(row, piece_ref.shape[0])], sem)
    copy.start()
    copy.wait()


def place(piece, row, total, buffer=None):
    args = (piece,) if buffer is None else (piece, buffer)
    return pl.pallas_call(
        functools.partial(place_kernel, row),
        out_shape=jax.ShapeDtypeStruct((total,) + piece.shape[1:], piece.dtype),
        in_specs=[pl.BlockSpec(memory_space=pl.ANY)] * len(args),
        out_specs=pl.BlockSpec(memory_space=pl.ANY),
        scratch_shapes=[pltpu.SemaphoreType.DMA],
        input_output_aliases={} if buffer is None else {1: 0},
        name="place",
    )(*args)


def attend_kernel(table_ref, lengths_ref, q_ref, nk_ref, nv_ref, *refs):
    page_refs, out_ref = refs[:-1], refs[-1]
    session = pl.program_id(0)
    length = lengths_ref[session]
    rows = page_refs[0].shape[1]
    half = KVH * HD
    scale = 1.0 / jnp.sqrt(jnp.float32(HD))
    spots = lax.broadcasted_iota(jnp.int32, (1, rows * len(page_refs)), 1)
    visible = spots < length
    for head in range(KVH):
        lanes = pl.ds(head * HD, HD)
        value_lanes = pl.ds(half + head * HD, HD)
        query = q_ref[0, head]
        scores = jnp.concatenate(
            [
                lax.dot_general(
                    query,
                    page[0, :, lanes],
                    (((1,), (1,)), ((), ())),
                    preferred_element_type=jnp.float32,
                )
                for page in page_refs
            ],
            axis=1,
        )
        scores = jnp.where(visible, scores * scale, jnp.float32(-1e30))
        own = (
            jnp.sum(
                query.astype(jnp.float32) * nk_ref[0, head].astype(jnp.float32),
                axis=1,
                keepdims=True,
            )
            * scale
        )
        highest = jnp.maximum(jnp.max(scores, axis=1, keepdims=True), own)
        expo = jnp.exp(scores - highest)
        own_expo = jnp.exp(own - highest)
        denominator = jnp.sum(expo, axis=1, keepdims=True) + own_expo
        weights = (expo / denominator).astype(jnp.bfloat16)
        own_weight = (own_expo / denominator).astype(jnp.bfloat16).astype(jnp.float32)
        result = own_weight * nv_ref[0, head].astype(jnp.float32)
        for at, page in enumerate(page_refs):
            result = result + jnp.dot(
                weights[:, at * rows : (at + 1) * rows],
                page[0, :, value_lanes],
                preferred_element_type=jnp.float32,
            )
        out_ref[0, head] = result.astype(jnp.bfloat16)


def attend(kv_pool, page_table, lengths, query, new_kv):
    sessions, pages = page_table.shape
    rows = STEPS * GRP
    queries = query.reshape(STEPS, sessions, KVH, GRP, HD).transpose(1, 2, 0, 3, 4)
    queries = queries.reshape(sessions, KVH, rows, HD)
    fresh = new_kv.reshape(STEPS, sessions, 2, KVH, 1, HD).transpose(2, 1, 3, 0, 4, 5)
    fresh = jnp.broadcast_to(fresh, (2, sessions, KVH, STEPS, GRP, HD))
    fresh = fresh.reshape(2, sessions, KVH, rows, HD)
    small = pl.BlockSpec((1, KVH, rows, HD), lambda s, table, lens: (s, 0, 0, 0))
    page_specs = [
        pl.BlockSpec((1,) + kv_pool.shape[1:], lambda s, table, lens, k=k: (table[s, k], 0, 0))
        for k in range(pages)
    ]
    return pl.pallas_call(
        attend_kernel,
        out_shape=jax.ShapeDtypeStruct((sessions, KVH, rows, HD), jnp.bfloat16),
        grid_spec=pltpu.PrefetchScalarGridSpec(
            num_scalar_prefetch=2,
            grid=(sessions,),
            in_specs=[small, small, small] + page_specs,
            out_specs=small,
        ),
        compiler_params=pltpu.CompilerParams(vmem_limit_bytes=24 << 20),
        cost_estimate=pl.CostEstimate(
            flops=4 * sessions * KVH * rows * HD * pages * 128,
            bytes_accessed=sessions * pages * 128 * 2048 * 2,
            transcendentals=sessions * KVH * rows * pages * 128,
        ),
        name="attend",
    )(page_table, lengths, queries, fresh[0], fresh[1], *([kv_pool] * pages))


def body(kv_pool, page_table, lengths, query, new_kv, moves):
    count = lax.axis_size("inst")
    sessions, pages = page_table.shape
    total = REACH * pages
    packed = pack(moves, page_table, kv_pool)
    query, new_kv, *packed = lax.optimization_barrier((query, new_kv, *packed))
    if count % 4 == 0:
        hops = relay_pairs(count)
    else:
        hops = (shift_pairs(count, 1),)
    near = send(packed[0], hops[0])
    far = send(packed[2], shift_pairs(count, 3))
    middle = send(packed[1], shift_pairs(count, 2))
    for hop in hops[1:]:
        near = send(near, hop)
    full = attend(kv_pool, page_table, lengths, query, new_kv)
    full = full.reshape(sessions, KVH, STEPS, GRP, HD).transpose(2, 0, 1, 3, 4)
    full = full.reshape(STEPS, sessions, HQ * HD)
    second = jnp.where((moves > 0)[:, None], jnp.zeros_like(full[1]), full[1])
    attended = jnp.stack([full[0], second])
    guests = []
    for offset in range(1, REACH + 1):
        leaving = jnp.argmax(moves == offset)
        row = lax.dynamic_slice_in_dim(full[1], leaving, 1, axis=0)
        guests.append(send(row, shift_pairs(count, offset)))
    guest_attended = jnp.concatenate(guests, axis=0)
    moved = place(far, 2 * pages, total)
    moved = place(near, 0, total, moved)
    moved = place(middle, pages, total, moved)
    return attended, guest_attended, moved


def solution(mesh):
    return jax.shard_map(
        body,
        mesh=mesh,
        in_specs=(
            P(("group", "inst"), None, None),
            P(("group", "inst"), None),
            P(("group", "inst")),
            P(None, ("group", "inst"), None),
            P(None, ("group", "inst"), None),
            P(("group", "inst")),
        ),
        out_specs=(
            P(None, ("group", "inst"), None),
            P(("group", "inst"), None),
            P(("group", "inst"), None, None),
        ),
        check_vma=False,
    )
```

time: 140 us -> 408 us (2.91)
  the two profiles are of different devices: /device:TPU:0 before, /device:TPU:18 now
where the time goes in v1:
time: 408 us; the launch traced here: 407 us
  Pallas kernels  304 us (75%)
  waiting for transfers between devices  65.3 us (16%)
  starting transfers between devices  20.6 us (5%)
  between operations  6.31 us (2%)
  local copies, waits for them, and re-layouts  5.64 us (1%)
  other arithmetic  5.52 us (1%)
    pallas_call x3, Pallas kernels, place(): pl.pallas_call(functools.partial(place_kernel, row), out_shape=jax.ShapeD...  146 us
    pallas_call x1, Pallas kernels, pack(): pl.pallas_call(pack_kernel, out_shape=(piece,) * REACH, in_specs=[pl.Bloc...  145 us
    ppermute x7, waiting for transfers between devices, send(): return lax.ppermute(value, 'inst', pairs)  65.3 us
    ppermute x7, starting transfers between devices, send(): return lax.ppermute(value, 'inst', pairs)  20.6 us
    pallas_call x1, Pallas kernels, attend(): pl.pallas_call(attend_kernel, out_shape=jax.ShapeDtypeStruct((sessions, K...  12.6 us
  transfers between devices with their start and end apart: 7, of which 1 were waited for; matrix products, arithmetic and copies ran while one was open for 0% of the time, Pallas kernels for 24%

profile of v1, /device:TPU:18, one launch (start us, length us, event | category | flops | bytes accessed | tf_op | source)
XLA Modules:
  0.0 407.2 jit_solution(10917744819733476541)
XLA Ops:
  0.6 1.3 compare_reduce_fusion.2
  1.9 1.3 compare_reduce_fusion
  5.6 1.3 compare_reduce_fusion.1
  8.2 0.0 copy-start.6
  8.2 0.0 copy-start.5
  8.2 0.0 copy-start.1
  8.2 0.0 copy-start.2
  8.2 145.0 %pack.1 = (bf16[3,128,2048]{2,1,0:T(8,128)(2,1)}, bf16[3,128,2048]{2,1,0:T(8,128)(2,1)}, bf16[3,128,2048]{2,1,0:T(8,128)(2,1)}) custom-call(s32[4]{0:T(128)} %moves_ref.1, s32[4,3]{1,0:T(4,128)} %table_ref.3, bf16[12,128,2048]{2,1,0:T(8,128)(2,1)} %refs_2_.1), custom_call_target="tpu_custom_call" | custom-call | tf_op jit(solution)/shard_map/pack/pallas_call | solution.py:55
  153.2 0.0 copy-done.6
  153.3 0.0 copy-done.5
  153.3 0.2 reshape.63
  153.6 0.0 copy-done.1
  153.6 0.0 copy-done.2
  153.6 0.0 copy-start
  153.6 2.8 copy-done
  156.4 0.0 copy-start.7
  156.4 12.6 %attend.1 = bf16[4,8,16,128]{3,2,1,0:T(8,128)(2,1)S(1)} custom-call(s32[4,3]{1,0:T(4,128)S(1)} %copy-done.1, s32[4]{0:T(128)S(1)} %copy-done.2, bf16[4,8,16,128]{3,2,1,0:T(8,128)(2,1)S(1)} %bitcast.32, bf16[4,8,16,128]{3,2,1,0:T(8,128)(2,1)S(1)} %get-tuple-element.34.nk_ref, bf16[4,8,16,128]{3,2,1,0:T(8,128)(2,1)S(1)} %get-tuple-element.33.nv_ref, ...), custom_call_target="tpu_custom_call" | custom-call | flops 100663296 | bytes 6291456 | tf_op jit(solution)/shard_map/attend/pallas_call | solution.py:152
  169.1 0.1 copy.18
  170.9 0.1 constant_dynamic-slice_fusion.2
  171.1 0.1 collective-permute-start
  171.1 2.7 collective-permute-start.2
  173.9 0.0 collective-permute-start.1
  173.9 1.7 collective-permute-start.3
  175.6 0.0 collective-permute-start.4
  175.6 0.0 copy-done.7
  175.6 0.1 broadcast_select_fusion
  175.7 0.0 collective-permute-done
  175.7 2.8 collective-permute-start.6
  178.5 65.2 %collective-permute-done.4 = bf16[3,128,2048]{2,1,0:T(8,128)(2,1)} collective-permute-done((bf16[3,128,2048]{2,1,0:T(8,128)(2,1)}, bf16[3,128,2048]{2,1,0:T(8,128)(2,1)}, u32[]{:S(2)}, u32[]{:S(2)}) %collective-permute-start.4) | collective-permute-done | bytes 1572896 | tf_op jit(solution)/shard_map/ppermute | solution.py:19
  243.8 13.3 %collective-permute-start.5 = (bf16[3,128,2048]{2,1,0:T(8,128)(2,1)}, bf16[3,128,2048]{2,1,0:T(8,128)(2,1)}, u32[]{:S(2)}, u32[]{:S(2)}) collective-permute-start(bf16[3,128,2048]{2,1,0:T(8,128)(2,1)} %collective-permute-done.4), channel_id=1, source_target_pairs={{0,4},{1,1},{2,2},{3,3},{4,8},{5,5},{6,6},{7,7},{8,12},{9,9},{10,1... | collective-permute-start | bytes 4718600 | tf_op jit(solution)/shard_map/ppermute | solution.py:19
  257.0 0.7 pad_maximum_fusion
  257.8 0.0 collective-permute-done.2
  257.8 0.0 collective-permute-done.1
  257.8 0.8 pad_maximum_fusion.1
  258.6 0.0 collective-permute-done.6.piece_ref
  258.6 0.0 copy-start.3
  258.6 1.1 copy-done.3
  259.7 48.8 %place.3.refs_0_ = bf16[9,128,2048]{2,1,0:T(8,128)(2,1)} custom-call(bf16[3,128,2048]{2,1,0:T(8,128)(2,1)} %copy-done.3), custom_call_target="tpu_custom_call" | custom-call | tf_op jit(solution)/shard_map/place/pallas_call | solution.py:78
  308.5 0.0 collective-permute-done.5.piece_ref
  308.5 48.8 %place.4.refs_0_ = bf16[9,128,2048]{2,1,0:T(8,128)(2,1)} custom-call(bf16[3,128,2048]{2,1,0:T(8,128)(2,1)} %collective-permute-done.5.piece_ref, bf16[9,128,2048]{2,1,0:T(8,128)(2,1)} %place.3.refs_0_), custom_call_target="tpu_custom_call", output_to_operand_aliasing={{}: (1, {})} | custom-call | tf_op jit(solution)/shard_map/place/pallas_call | solution.py:78
  357.2 0.0 collective-permute-done.3.piece_ref
  357.3 0.0 copy-start.4
  357.3 1.1 copy-done.4
  358.4 48.8 %place.5 = bf16[9,128,2048]{2,1,0:T(8,128)(2,1)} custom-call(bf16[3,128,2048]{2,1,0:T(8,128)(2,1)} %copy-done.4, bf16[9,128,2048]{2,1,0:T(8,128)(2,1)} %place.4.refs_0_), custom_call_target="tpu_custom_call", output_to_operand_aliasing={{}: (1, {})} | custom-call | tf_op jit(solution)/shard_map/place/pallas_call | solution.py:78
  (10 shorter events, 0.2 us)
Async XLA Ops:
  8.2 145.0 %copy-start.6 = (bf16[2,4,2048]{2,1,0:T(4,128)(2,1)S(1)}, bf16[2,4,2048]{2,1,0:T(4,128)(2,1)}, u32[]{:S(2)}) copy-start(bf16[2,4,2048]{2,1,0:T(4,128)(2,1)} %param.10) | copy-start | bytes 98308
  8.2 145.1 %copy-start.5 = (bf16[2,4,8192]{2,1,0:T(4,128)(2,1)S(1)}, bf16[2,4,8192]{2,1,0:T(4,128)(2,1)}, u32[]{:S(2)}) copy-start(bf16[2,4,8192]{2,1,0:T(4,128)(2,1)} %param.9) | copy-start | bytes 393220
  8.2 145.4 %copy-start.1 = (s32[4,3]{1,0:T(4,128)S(1)}, s32[4,3]{1,0:T(4,128)}, u32[]{:S(2)}) copy-start(s32[4,3]{1,0:T(4,128)} %table_ref.3) | copy-start | bytes 148
  8.2 145.4 %copy-start.2 = (s32[4]{0:T(128)S(1)}, s32[4]{0:T(128)}, u32[]{:S(2)}) copy-start(s32[4]{0:T(128)} %lengths_ref.1) | copy-start | bytes 52
  153.6 2.8 copy-start
  156.4 19.2 %copy-start.7 = (s32[4]{0:T(128)S(1)}, s32[4]{0:T(128)}, u32[]{:S(2)}) copy-start(s32[4]{0:T(128)} %moves_ref.1) | copy-start | bytes 52
  171.1 4.7 %collective-permute-start = (bf16[1,8192]{1,0:T(2,128)(2,1)S(1)}, bf16[1,8192]{1,0:T(2,128)(2,1)S(1)}, u32[]{:S(2)}, u32[]{:S(2)}) collective-permute-start(bf16[1,8192]{1,0:T(2,128)(2,1)S(1)} %get-tuple-element.28), channel_id=1, source_target_pairs={{0,1},{1,2},{2,3},{3,4},{4,5},{5,6},{6,7},{7,8},{8,9},{9,10},{10,1... | collective-permute-start | bytes 49160 | tf_op jit(solution)/shard_map/ppermute | solution.py:19
  171.1 86.7 %collective-permute-start.2 = (bf16[1,8192]{1,0:T(2,128)(2,1)S(1)}, bf16[1,8192]{1,0:T(2,128)(2,1)S(1)}, u32[]{:S(2)}, u32[]{:S(2)}) collective-permute-start(bf16[1,8192]{1,0:T(2,128)(2,1)S(1)} %get-tuple-element.29), channel_id=1, source_target_pairs={{0,3},{1,4},{2,5},{3,6},{4,7},{5,8},{6,9},{7,10},{8,11},{9,12},{10... | collective-permute-start | bytes 49160 | tf_op jit(solution)/shard_map/ppermute | solution.py:19
  173.9 83.9 %collective-permute-start.1 = (bf16[1,8192]{1,0:T(2,128)(2,1)S(1)}, bf16[1,8192]{1,0:T(2,128)(2,1)S(1)}, u32[]{:S(2)}, u32[]{:S(2)}) collective-permute-start(bf16[1,8192]{1,0:T(2,128)(2,1)S(1)} %get-tuple-element.30), channel_id=1, source_target_pairs={{0,2},{1,3},{2,4},{3,5},{4,6},{5,7},{6,8},{7,9},{8,10},{9,11},{10,... | collective-permute-start | bytes 49160 | tf_op jit(solution)/shard_map/ppermute | solution.py:19
  173.9 183.4 %collective-permute-start.3 = (bf16[3,128,2048]{2,1,0:T(8,128)(2,1)}, bf16[3,128,2048]{2,1,0:T(8,128)(2,1)S(1)}, u32[]{:S(2)}, u32[]{:S(2)}) collective-permute-start(bf16[3,128,2048]{2,1,0:T(8,128)(2,1)} %get-tuple-element.22), channel_id=1, source_target_pairs={{0,2},{1,3},{2,4},{3,5},{4,6},{5,7},{6,8},{7,9},{8,10},{9,11},{10,... | collective-permute-start | bytes 4718600 | tf_op jit(solution)/shard_map/ppermute | solution.py:19
  175.6 68.2 %collective-permute-start.4 = (bf16[3,128,2048]{2,1,0:T(8,128)(2,1)}, bf16[3,128,2048]{2,1,0:T(8,128)(2,1)}, u32[]{:S(2)}, u32[]{:S(2)}) collective-permute-start(bf16[3,128,2048]{2,1,0:T(8,128)(2,1)} %get-tuple-element.23), channel_id=1, source_target_pairs={{0,1},{1,2},{2,3},{3,0},{4,5},{5,6},{6,7},{7,4},{8,9},{9,10},{10,1... | collective-permute-start | bytes 4718600 | tf_op jit(solution)/shard_map/ppermute | solution.py:19
  175.7 82.8 %collective-permute-start.6 = (bf16[3,128,2048]{2,1,0:T(8,128)(2,1)}, bf16[3,128,2048]{2,1,0:T(8,128)(2,1)S(1)}, u32[]{:S(2)}, u32[]{:S(2)}) collective-permute-start(bf16[3,128,2048]{2,1,0:T(8,128)(2,1)} %get-tuple-element.24), channel_id=1, source_target_pairs={{0,3},{1,4},{2,5},{3,6},{4,7},{5,8},{6,9},{7,10},{8,11},{9,12},{10... | collective-permute-start | bytes 4718600 | tf_op jit(solution)/shard_map/ppermute | solution.py:19
  243.8 64.7 %collective-permute-start.5 = (bf16[3,128,2048]{2,1,0:T(8,128)(2,1)}, bf16[3,128,2048]{2,1,0:T(8,128)(2,1)}, u32[]{:S(2)}, u32[]{:S(2)}) collective-permute-start(bf16[3,128,2048]{2,1,0:T(8,128)(2,1)} %collective-permute-done.4), channel_id=1, source_target_pairs={{0,4},{1,1},{2,2},{3,3},{4,8},{5,5},{6,6},{7,7},{8,12},{9,9},{10,1... | collective-permute-start | bytes 4718600 | tf_op jit(solution)/shard_map/ppermute | solution.py:19
  258.6 1.1 copy-start.3
  357.3 1.2 copy-start.4

commit v2 on v1

v2 whole, which is shorter than its diff:
```python
import functools

import jax
import jax.numpy as jnp
from jax import lax
from jax.experimental import pallas as pl
from jax.experimental.pallas import tpu as pltpu
from jax.sharding import PartitionSpec as P

HQ = 64
KVH = 8
HD = 128
REACH = 3
GRP = 8
STEPS = 2
SMALL = pl.CostEstimate(flops=0, bytes_accessed=0, transcendentals=0)
LITTLE = 4 << 20


def send(value, pairs):
    return lax.ppermute(value, "inst", pairs)


def shift_pairs(count, steps):
    return [(source, (source + steps) % count) for source in range(count)]


def relay_pairs(count):
    first = [(i, i - 3 if i % 4 == 3 else i + 1) for i in range(count)]
    second = [(i, (i + 4) % count if i % 4 == 0 else i) for i in range(count)]
    return first, second


def pack_kernel(offsets, moves_ref, table_ref, pool_ref, *refs):
    outs, held, in_sems, out_sems = refs[: len(offsets)], *refs[-3:]
    spots, reads, writes = [], [], []
    for at, offset in enumerate(offsets):
        mover = jnp.int32(0)
        for session in range(1, table_ref.shape[0]):
            mover = jnp.where(moves_ref[session] == offset, jnp.int32(session), mover)
        for page in range(table_ref.shape[1]):
            spots.append((at, page))
            reads.append(
                pltpu.make_async_copy(
                    pool_ref.at[table_ref[mover, page]], held.at[at, page], in_sems.at[at, page]
                )
            )
            reads[-1].start()
    for (at, page), read in zip(spots, reads):
        read.wait()
        writes.append(
            pltpu.make_async_copy(held.at[at, page], outs[at].at[page], out_sems.at[at, page])
        )
        writes[-1].start()
    for write in writes:
        write.wait()


def pack(offsets, moves, page_table, kv_pool):
    pages = page_table.shape[1]
    count = len(offsets)
    piece = jax.ShapeDtypeStruct((pages,) + kv_pool.shape[1:], kv_pool.dtype)
    return pl.pallas_call(
        functools.partial(pack_kernel, offsets),
        out_shape=(piece,) * count,
        in_specs=[
            pl.BlockSpec(memory_space=pltpu.SMEM),
            pl.BlockSpec(memory_space=pltpu.SMEM),
            pl.BlockSpec(memory_space=pltpu.HBM),
        ],
        out_specs=(pl.BlockSpec(memory_space=pl.ANY),) * count,
        scratch_shapes=[
            pltpu.VMEM((count, pages) + kv_pool.shape[1:], kv_pool.dtype),
            pltpu.SemaphoreType.DMA((count, pages)),
            pltpu.SemaphoreType.DMA((count, pages)),
        ],
        compiler_params=pltpu.CompilerParams(vmem_limit_bytes=8 << 20),
        cost_estimate=SMALL,
        name="pack",
    )(moves, page_table, pltpu.with_memory_space_constraint(kv_pool, pltpu.HBM))


def place_kernel(row, piece_ref, *refs):
    out_ref, sem = refs[-2], refs[-1]
    copy = pltpu.make_async_copy(piece_ref, out_ref.at[pl.ds(row, piece_ref.shape[0])], sem)
    copy.start()
    copy.wait()


def place(piece, row, total, buffer=None):
    args = (pltpu.with_memory_space_constraint(piece, pltpu.VMEM),)
    if buffer is not None:
        args += (buffer,)
    return pl.pallas_call(
        functools.partial(place_kernel, row),
        out_shape=pltpu.HBM((total,) + piece.shape[1:], piece.dtype),
        in_specs=[
            pl.BlockSpec(memory_space=pltpu.VMEM),
            pl.BlockSpec(memory_space=pltpu.HBM),
        ][: len(args)],
        out_specs=pl.BlockSpec(memory_space=pltpu.HBM),
        scratch_shapes=[pltpu.SemaphoreType.DMA],
        input_output_aliases={} if buffer is None else {1: 0},
        compiler_params=pltpu.CompilerParams(vmem_limit_bytes=LITTLE),
        cost_estimate=SMALL,
        name="place",
    )(*args)


def attend_kernel(table_ref, lengths_ref, moves_ref, q_ref, nk_ref, nv_ref, *refs):
    page_refs, out_ref, guest_ref = refs[:-2], refs[-2], refs[-1]
    session = pl.program_id(0)
    length = lengths_ref[session]
    move = moves_ref[session]
    rows = page_refs[0].shape[1]
    half = KVH * HD
    scale = 1.0 / jnp.sqrt(jnp.float32(HD))
    spots = lax.broadcasted_iota(jnp.int32, (1, rows * len(page_refs)), 1)
    visible = spots < length
    for head in range(KVH):
        lanes = pl.ds(head * HD, HD)
        value_lanes = pl.ds(half + head * HD, HD)
        query = q_ref[0, head]
        scores = jnp.concatenate(
            [
                lax.dot_general(
                    query,
                    page[0, :, lanes],
                    (((1,), (1,)), ((), ())),
                    preferred_element_type=jnp.float32,
                )
                for page in page_refs
            ],
            axis=1,
        )
        scores = jnp.where(visible, scores * scale, jnp.float32(-1e30))
        own = (
            jnp.sum(
                query.astype(jnp.float32) * nk_ref[0, head].astype(jnp.float32),
                axis=1,
                keepdims=True,
            )
            * scale
        )
        highest = jnp.maximum(jnp.max(scores, axis=1, keepdims=True), own)
        expo = jnp.exp(scores - highest)
        own_expo = jnp.exp(own - highest)
        denominator = jnp.sum(expo, axis=1, keepdims=True) + own_expo
        weights = (expo / denominator).astype(jnp.bfloat16)
        own_weight = (own_expo / denominator).astype(jnp.bfloat16).astype(jnp.float32)
        result = own_weight * nv_ref[0, head].astype(jnp.float32)
        for at, page in enumerate(page_refs):
            result = result + jnp.dot(
                weights[:, at * rows : (at + 1) * rows],
                page[0, :, value_lanes],
                preferred_element_type=jnp.float32,
            )
        result = result.astype(jnp.bfloat16)
        heads = pl.ds(head * GRP, GRP)
        later = result[GRP:]
        out_ref[0, 0, heads] = result[:GRP]
        out_ref[1, 0, heads] = jnp.where(move > 0, jnp.zeros_like(later), later)

        @pl.when(move > 0)
        def _():
            guest_ref[jnp.maximum(move - 1, 0), heads] = later


def attend(kv_pool, page_table, lengths, moves, query, new_kv):
    sessions, pages = page_table.shape
    rows = STEPS * GRP
    queries = query.reshape(STEPS, sessions, KVH, GRP, HD).transpose(1, 2, 0, 3, 4)
    queries = queries.reshape(sessions, KVH, rows, HD)
    fresh = new_kv.reshape(STEPS, sessions, 2, KVH, 1, HD).transpose(2, 1, 3, 0, 4, 5)
    fresh = jnp.broadcast_to(fresh, (2, sessions, KVH, STEPS, GRP, HD))
    fresh = fresh.reshape(2, sessions, KVH, rows, HD)
    small = pl.BlockSpec((1, KVH, rows, HD), lambda s, *_: (s, 0, 0, 0))
    page_specs = [
        pl.BlockSpec((1,) + kv_pool.shape[1:], lambda s, table, *_, k=k: (table[s, k], 0, 0))
        for k in range(pages)
    ]
    return pl.pallas_call(
        attend_kernel,
        out_shape=(
            jax.ShapeDtypeStruct((STEPS, sessions, HQ, HD), jnp.bfloat16),
            jax.ShapeDtypeStruct((REACH, HQ, HD), jnp.bfloat16),
        ),
        grid_spec=pltpu.PrefetchScalarGridSpec(
            num_scalar_prefetch=3,
            grid=(sessions,),
            in_specs=[small, small, small] + page_specs,
            out_specs=(
                pl.BlockSpec((STEPS, 1, HQ, HD), lambda s, *_: (0, s, 0, 0)),
                pl.BlockSpec((REACH, HQ, HD), lambda s, *_: (0, 0, 0)),
            ),
        ),
        compiler_params=pltpu.CompilerParams(vmem_limit_bytes=24 << 20),
        cost_estimate=SMALL,
        name="attend",
    )(page_table, lengths, moves, queries, fresh[0], fresh[1], *([pltpu.with_memory_space_constraint(kv_pool, pltpu.HBM)] * pages))


def body(kv_pool, page_table, lengths, query, new_kv, moves):
    count = lax.axis_size("inst")
    sessions, pages = page_table.shape
    total = REACH * pages
    near, far = pack((1, 3), moves, page_table, kv_pool)
    near, far, table, query, new_kv = lax.optimization_barrier(
        (near, far, page_table, query, new_kv)
    )
    (middle,) = pack((2,), moves, table, kv_pool)
    full, leaving = attend(kv_pool, table, lengths, moves, query, new_kv)
    full, leaving, middle = lax.optimization_barrier((full, leaving, middle))
    if count % 4 == 0:
        hops = relay_pairs(count)
    else:
        hops = (shift_pairs(count, 1),)
    near = send(near, hops[0])
    far = send(far, shift_pairs(count, 3))
    attended = full.reshape(STEPS, sessions, HQ * HD)
    leaving = leaving.reshape(REACH, HQ * HD)
    middle = send(middle, shift_pairs(count, 2))
    near, leaving = lax.optimization_barrier((near, leaving))
    guests = [
        send(leaving[offset - 1 : offset], shift_pairs(count, offset))
        for offset in range(1, REACH + 1)
    ]
    near, far = lax.optimization_barrier((near, far))
    for hop in hops[1:]:
        near = send(near, hop)
    guest_attended = jnp.concatenate(guests, axis=0)
    moved = place(far, 2 * pages, total)
    moved = place(near, 0, total, moved)
    moved = place(middle, pages, total, moved)
    return attended, guest_attended, moved


def solution(mesh):
    return jax.shard_map(
        body,
        mesh=mesh,
        in_specs=(
            P(("group", "inst"), None, None),
            P(("group", "inst"), None),
            P(("group", "inst")),
            P(None, ("group", "inst"), None),
            P(None, ("group", "inst"), None),
            P(("group", "inst")),
        ),
        out_specs=(
            P(None, ("group", "inst"), None),
            P(("group", "inst"), None),
            P(("group", "inst"), None, None),
        ),
        check_vma=False,
    )
```

time: 408 us -> 89.2 us (0.22)
  the two profiles are of different devices: /device:TPU:18 before, /device:TPU:0 now
where the time goes in v2:
time: 89.2 us; the launch traced here: 88.2 us
  Pallas kernels  30 us (34%)
  waiting for transfers between devices  29 us (33%)
  starting transfers between devices  25.3 us (28%)
  local copies, waits for them, and re-layouts  2.44 us (3%)
    ppermute x7, waiting for transfers between devices, send(): return lax.ppermute(value, 'inst', pairs)  29 us
    ppermute x7, starting transfers between devices, send(): return lax.ppermute(value, 'inst', pairs)  25.3 us
    pallas_call x1, Pallas kernels, attend(): pl.pallas_call(attend_kernel, out_shape=(jax.ShapeDtypeStruct((STEPS, ses...  18.3 us
    pallas_call x3, Pallas kernels, place(): pl.pallas_call(functools.partial(place_kernel, row), out_shape=pltpu.HBM(...  6.27 us
    pallas_call x2, Pallas kernels, pack(): pl.pallas_call(functools.partial(pack_kernel, offsets), out_shape=(piece,...  5.42 us
  transfers between devices with their start and end apart: 7, of which 4 were waited for; matrix products, arithmetic and copies ran while one was open for 2% of the time, Pallas kernels for 27%

profile of v2, /device:TPU:0, one launch (start us, length us, event | category | flops | bytes accessed | tf_op | source)
XLA Modules:
  0.0 88.2 jit_solution(9697010051153643375)
XLA Ops:
  0.6 0.0 copy-start
  0.6 0.7 copy-done
  1.3 0.0 copy-start.2
  1.3 0.7 copy-done.2
  2.0 0.0 copy-start.6
  2.0 0.0 copy-start.5
  2.0 0.0 copy-start.1
  2.0 0.0 copy-start.3
  2.0 3.4 %pack.2 = (bf16[3,128,2048]{2,1,0:T(8,128)(2,1)}, bf16[3,128,2048]{2,1,0:T(8,128)(2,1)}) custom-call(s32[4]{0:T(128)S(1)} %copy-done.2, s32[4,3]{1,0:T(4,128)S(1)} %copy-done, bf16[12,128,2048]{2,1,0:T(8,128)(2,1)} %pool_ref.3), custom_call_target="tpu_custom_call" | custom-call | tf_op jit(solution)/shard_map/pack/pallas_call | solution.py:63
  5.4 0.5 collective-permute-start
  5.9 2.0 %collective-permute-start.5 = (bf16[3,128,2048]{2,1,0:T(8,128)(2,1)}, bf16[3,128,2048]{2,1,0:T(8,128)(2,1)S(1)}, u32[]{:S(2)}, u32[]{:S(2)}) collective-permute-start(bf16[3,128,2048]{2,1,0:T(8,128)(2,1)} %get-tuple-element.32), channel_id=1, source_target_pairs={{0,3},{1,4},{2,5},{3,6},{4,7},{5,8},{6,9},{7,10},{8,11},{9,12},{10... | collective-permute-start | bytes 4718600 | tf_op jit(solution)/shard_map/ppermute | solution.py:21
  7.9 0.0 copy-done.6
  8.0 0.0 copy-done.5
  8.0 0.2 reshape.34
  8.2 0.0 copy-done.1
  8.2 0.0 copy-done.3
  8.2 0.0 copy-start.4
  8.2 2.0 %pack.3 = bf16[3,128,2048]{2,1,0:T(8,128)(2,1)S(1)} custom-call(s32[4]{0:T(128)S(1)} %copy-done.3, s32[4,3]{1,0:T(4,128)S(1)} %copy-done.1, bf16[12,128,2048]{2,1,0:T(8,128)(2,1)} %pool_ref.3), custom_call_target="tpu_custom_call" | custom-call | tf_op jit(solution)/shard_map/pack/pallas_call | solution.py:63
  10.3 0.0 copy-done.4
  10.3 18.3 %attend.1 = (bf16[2,4,64,128]{3,2,1,0:T(8,128)(2,1)S(1)}, bf16[3,64,128]{2,1,0:T(8,128)(2,1)S(1)}) custom-call(s32[4,3]{1,0:T(4,128)S(1)} %copy-done.1, s32[4]{0:T(128)S(1)} %copy-done.4, s32[4]{0:T(128)S(1)} %copy-done.3, bf16[4,8,16,128]{3,2,1,0:T(8,128)(2,1)S(1)} %bitcast.20, bf16[4,8,16,128]{3,2,1,0:T(8,128)(2,1)S(1)} %get-tuple-element.41.nk_ref, ...), custom_call_target="tpu_custom_call" | custom-call | tf_op jit(solution)/shard_map/attend/pallas_call | solution.py:182
  28.6 3.3 %collective-permute-start.4 = (bf16[3,128,2048]{2,1,0:T(8,128)(2,1)S(1)}, bf16[3,128,2048]{2,1,0:T(8,128)(2,1)}, u32[]{:S(2)}, u32[]{:S(2)}) collective-permute-start(bf16[3,128,2048]{2,1,0:T(8,128)(2,1)S(1)} %pack.3), channel_id=1, source_target_pairs={{0,2},{1,3},{2,4},{3,5},{4,6},{5,7},{6,8},{7,9},{8,10},{9,11},{10,... | collective-permute-start | bytes 4718600 | tf_op jit(solution)/shard_map/ppermute | solution.py:21
  31.9 5.8 %collective-permute-done = bf16[3,128,2048]{2,1,0:T(8,128)(2,1)} collective-permute-done((bf16[3,128,2048]{2,1,0:T(8,128)(2,1)}, bf16[3,128,2048]{2,1,0:T(8,128)(2,1)}, u32[]{:S(2)}, u32[]{:S(2)}) %collective-permute-start) | collective-permute-done | bytes 1572896 | tf_op jit(solution)/shard_map/ppermute | solution.py:21
  37.7 5.2 %collective-permute-done.5.piece_ref = bf16[3,128,2048]{2,1,0:T(8,128)(2,1)S(1)} collective-permute-done((bf16[3,128,2048]{2,1,0:T(8,128)(2,1)}, bf16[3,128,2048]{2,1,0:T(8,128)(2,1)S(1)}, u32[]{:S(2)}, u32[]{:S(2)}) %collective-permute-start.5) | collective-permute-done | bytes 1572896 | tf_op jit(solution)/shard_map/ppermute | solution.py:21
  43.0 4.2 %collective-permute-start.6 = (bf16[3,128,2048]{2,1,0:T(8,128)(2,1)}, bf16[3,128,2048]{2,1,0:T(8,128)(2,1)}, u32[]{:S(2)}, u32[]{:S(2)}) collective-permute-start(bf16[3,128,2048]{2,1,0:T(8,128)(2,1)} %collective-permute-done), channel_id=1, source_target_pairs={{0,4},{1,1},{2,2},{3,3},{4,8},{5,5},{6,6},{7,7},{8,12},{9,9},{10,1... | collective-permute-start | bytes 4718600 | tf_op jit(solution)/shard_map/ppermute | solution.py:21
  47.2 0.1 fusion
  47.3 14.3 %collective-permute-start.1 = (bf16[1,8192]{1,0:T(2,128)(2,1)S(1)}, bf16[1,8192]{1,0:T(2,128)(2,1)S(1)}, u32[]{:S(2)}, u32[]{:S(2)}) collective-permute-start(bf16[1,8192]{1,0:T(2,128)(2,1)S(1)} %get-tuple-element.35), channel_id=1, source_target_pairs={{0,1},{1,2},{2,3},{3,4},{4,5},{5,6},{6,7},{7,8},{8,9},{9,10},{10,1... | collective-permute-start | bytes 49160 | tf_op jit(solution)/shard_map/ppermute | solution.py:21
  61.6 0.0 collective-permute-start.3
  61.6 0.9 %collective-permute-start.2 = (bf16[1,8192]{1,0:T(2,128)(2,1)S(1)}, bf16[1,8192]{1,0:T(2,128)(2,1)S(1)}, u32[]{:S(2)}, u32[]{:S(2)}) collective-permute-start(bf16[1,8192]{1,0:T(2,128)(2,1)S(1)} %get-tuple-element.37), channel_id=1, source_target_pairs={{0,2},{1,3},{2,4},{3,5},{4,6},{5,7},{6,8},{7,9},{8,10},{9,11},{10,... | collective-permute-start | bytes 49160 | tf_op jit(solution)/shard_map/ppermute | solution.py:21
  62.5 0.7 reshape.37
  63.2 1.1 %place.3.refs_0_ = bf16[9,128,2048]{2,1,0:T(8,128)(2,1)} custom-call(bf16[3,128,2048]{2,1,0:T(8,128)(2,1)S(1)} %collective-permute-done.5.piece_ref), custom_call_target="tpu_custom_call" | custom-call | tf_op jit(solution)/shard_map/place/pallas_call | solution.py:94
  64.4 15.4 %collective-permute-done.1 = bf16[1,8192]{1,0:T(2,128)(2,1)S(1)} collective-permute-done((bf16[1,8192]{1,0:T(2,128)(2,1)S(1)}, bf16[1,8192]{1,0:T(2,128)(2,1)S(1)}, u32[]{:S(2)}, u32[]{:S(2)}) %collective-permute-start.1) | collective-permute-done | bytes 16416 | tf_op jit(solution)/shard_map/ppermute | solution.py:21
  79.7 0.0 collective-permute-done.3
  79.7 2.6 %collective-permute-done.2 = bf16[1,8192]{1,0:T(2,128)(2,1)S(1)} collective-permute-done((bf16[1,8192]{1,0:T(2,128)(2,1)S(1)}, bf16[1,8192]{1,0:T(2,128)(2,1)S(1)}, u32[]{:S(2)}, u32[]{:S(2)}) %collective-permute-start.2) | collective-permute-done | bytes 16416 | tf_op jit(solution)/shard_map/ppermute | solution.py:21
  82.3 0.7 pad_maximum_fusion
  83.0 0.0 collective-permute-done.6.piece_ref
  83.0 2.6 %place.4.refs_0_ = bf16[9,128,2048]{2,1,0:T(8,128)(2,1)} custom-call(bf16[3,128,2048]{2,1,0:T(8,128)(2,1)} %collective-permute-done.6.piece_ref, bf16[9,128,2048]{2,1,0:T(8,128)(2,1)} %place.3.refs_0_), custom_call_target="tpu_custom_call", output_to_operand_aliasing={{}: (1, {})} | custom-call | tf_op jit(solution)/shard_map/place/pallas_call | solution.py:94
  85.6 0.0 collective-permute-done.4.piece_ref
  85.6 2.6 %place.5 = bf16[9,128,2048]{2,1,0:T(8,128)(2,1)} custom-call(bf16[3,128,2048]{2,1,0:T(8,128)(2,1)} %collective-permute-done.4.piece_ref, bf16[9,128,2048]{2,1,0:T(8,128)(2,1)} %place.4.refs_0_), custom_call_target="tpu_custom_call", output_to_operand_aliasing={{}: (1, {})} | custom-call | tf_op jit(solution)/shard_map/place/pallas_call | solution.py:94
  (7 shorter events, 0.2 us)
Async XLA Ops:
  0.6 0.7 copy-start
  1.3 0.7 copy-start.2
  2.0 5.9 %copy-start.6 = (bf16[2,4,2048]{2,1,0:T(4,128)(2,1)S(1)}, bf16[2,4,2048]{2,1,0:T(4,128)(2,1)}, u32[]{:S(2)}) copy-start(bf16[2,4,2048]{2,1,0:T(4,128)(2,1)} %param.10) | copy-start | bytes 98308
  2.0 6.0 %copy-start.5 = (bf16[2,4,8192]{2,1,0:T(4,128)(2,1)S(1)}, bf16[2,4,8192]{2,1,0:T(4,128)(2,1)}, u32[]{:S(2)}) copy-start(bf16[2,4,8192]{2,1,0:T(4,128)(2,1)} %param.9) | copy-start | bytes 393220
  2.0 6.2 %copy-start.1 = (s32[4,3]{1,0:T(4,128)S(1)}, s32[4,3]{1,0:T(4,128)}, u32[]{:S(2)}) copy-start(s32[4,3]{1,0:T(4,128)} %table_ref.3) | copy-start | bytes 148
  2.0 6.2 %copy-start.3 = (s32[4]{0:T(128)S(1)}, s32[4]{0:T(128)}, u32[]{:S(2)}) copy-start(s32[4]{0:T(128)} %moves_ref.5) | copy-start | bytes 52
  5.4 32.3 %collective-permute-start = (bf16[3,128,2048]{2,1,0:T(8,128)(2,1)}, bf16[3,128,2048]{2,1,0:T(8,128)(2,1)}, u32[]{:S(2)}, u32[]{:S(2)}) collective-permute-start(bf16[3,128,2048]{2,1,0:T(8,128)(2,1)} %get-tuple-element.27), channel_id=1, source_target_pairs={{0,1},{1,2},{2,3},{3,0},{4,5},{5,6},{6,7},{7,4},{8,9},{9,10},{10,1... | collective-permute-start | bytes 4718600 | tf_op jit(solution)/shard_map/ppermute | solution.py:21
  5.9 37.1 %collective-permute-start.5 = (bf16[3,128,2048]{2,1,0:T(8,128)(2,1)}, bf16[3,128,2048]{2,1,0:T(8,128)(2,1)S(1)}, u32[]{:S(2)}, u32[]{:S(2)}) collective-permute-start(bf16[3,128,2048]{2,1,0:T(8,128)(2,1)} %get-tuple-element.32), channel_id=1, source_target_pairs={{0,3},{1,4},{2,5},{3,6},{4,7},{5,8},{6,9},{7,10},{8,11},{9,12},{10... | collective-permute-start | bytes 4718600 | tf_op jit(solution)/shard_map/ppermute | solution.py:21
  8.2 2.1 %copy-start.4 = (s32[4]{0:T(128)S(1)}, s32[4]{0:T(128)}, u32[]{:S(2)}) copy-start(s32[4]{0:T(128)} %lengths_ref.1) | copy-start | bytes 52
  28.6 57.0 %collective-permute-start.4 = (bf16[3,128,2048]{2,1,0:T(8,128)(2,1)S(1)}, bf16[3,128,2048]{2,1,0:T(8,128)(2,1)}, u32[]{:S(2)}, u32[]{:S(2)}) collective-permute-start(bf16[3,128,2048]{2,1,0:T(8,128)(2,1)S(1)} %pack.3), channel_id=1, source_target_pairs={{0,2},{1,3},{2,4},{3,5},{4,6},{5,7},{6,8},{7,9},{8,10},{9,11},{10,... | collective-permute-start | bytes 4718600 | tf_op jit(solution)/shard_map/ppermute | solution.py:21
  43.0 40.1 %collective-permute-start.6 = (bf16[3,128,2048]{2,1,0:T(8,128)(2,1)}, bf16[3,128,2048]{2,1,0:T(8,128)(2,1)}, u32[]{:S(2)}, u32[]{:S(2)}) collective-permute-start(bf16[3,128,2048]{2,1,0:T(8,128)(2,1)} %collective-permute-done), channel_id=1, source_target_pairs={{0,4},{1,1},{2,2},{3,3},{4,8},{5,5},{6,6},{7,7},{8,12},{9,9},{10,1... | collective-permute-start | bytes 4718600 | tf_op jit(solution)/shard_map/ppermute | solution.py:21
  47.3 32.5 %collective-permute-start.1 = (bf16[1,8192]{1,0:T(2,128)(2,1)S(1)}, bf16[1,8192]{1,0:T(2,128)(2,1)S(1)}, u32[]{:S(2)}, u32[]{:S(2)}) collective-permute-start(bf16[1,8192]{1,0:T(2,128)(2,1)S(1)} %get-tuple-element.35), channel_id=1, source_target_pairs={{0,1},{1,2},{2,3},{3,4},{4,5},{5,6},{6,7},{7,8},{8,9},{9,10},{10,1... | collective-permute-start | bytes 49160 | tf_op jit(solution)/shard_map/ppermute | solution.py:21
  61.6 18.1 %collective-permute-start.3 = (bf16[1,8192]{1,0:T(2,128)(2,1)S(1)}, bf16[1,8192]{1,0:T(2,128)(2,1)S(1)}, u32[]{:S(2)}, u32[]{:S(2)}) collective-permute-start(bf16[1,8192]{1,0:T(2,128)(2,1)S(1)} %get-tuple-element.36), channel_id=1, source_target_pairs={{0,3},{1,4},{2,5},{3,6},{4,7},{5,8},{6,9},{7,10},{8,11},{9,12},{10... | collective-permute-start | bytes 49160 | tf_op jit(solution)/shard_map/ppermute | solution.py:21
  61.6 20.7 %collective-permute-start.2 = (bf16[1,8192]{1,0:T(2,128)(2,1)S(1)}, bf16[1,8192]{1,0:T(2,128)(2,1)S(1)}, u32[]{:S(2)}, u32[]{:S(2)}) collective-permute-start(bf16[1,8192]{1,0:T(2,128)(2,1)S(1)} %get-tuple-element.37), channel_id=1, source_target_pairs={{0,2},{1,3},{2,4},{3,5},{4,6},{5,7},{6,8},{7,9},{8,10},{9,11},{10,... | collective-permute-start | bytes 49160 | tf_op jit(solution)/shard_map/ppermute | solution.py:21

commit v3 on v2

v3 whole, which is shorter than its diff:
```python
import functools

import jax
import jax.numpy as jnp
from jax import lax
from jax.experimental import pallas as pl
from jax.experimental.pallas import tpu as pltpu
from jax.sharding import PartitionSpec as P

HQ = 64
KVH = 8
HD = 128
REACH = 3
GRP = 8
STEPS = 2
SMALL = pl.CostEstimate(flops=0, bytes_accessed=0, transcendentals=0)
LITTLE = 5 << 20
PARTS = 2


def send(value, pairs):
    return lax.ppermute(value, "inst", pairs)


def shift_pairs(count, steps):
    return [(source, (source + steps) % count) for source in range(count)]


def relay_pairs(count):
    first = [(i, i - 3 if i % 4 == 3 else i + 1) for i in range(count)]
    second = [(i, (i + 4) % count if i % 4 == 0 else i) for i in range(count)]
    return first, second


def pack_kernel(offsets, moves_ref, table_ref, pool_ref, *refs):
    outs, held, in_sems, out_sems = refs[: len(offsets)], *refs[-3:]
    spots, reads, writes = [], [], []
    for at, offset in enumerate(offsets):
        mover = jnp.int32(0)
        for session in range(1, table_ref.shape[0]):
            mover = jnp.where(moves_ref[session] == offset, jnp.int32(session), mover)
        for page in range(table_ref.shape[1]):
            spots.append((at, page))
            reads.append(
                pltpu.make_async_copy(
                    pool_ref.at[table_ref[mover, page]], held.at[at, page], in_sems.at[at, page]
                )
            )
            reads[-1].start()
    for (at, page), read in zip(spots, reads):
        read.wait()
        writes.append(
            pltpu.make_async_copy(held.at[at, page], outs[at].at[page], out_sems.at[at, page])
        )
        writes[-1].start()
    for write in writes:
        write.wait()


def pack(offsets, moves, page_table, kv_pool):
    pages = page_table.shape[1]
    count = len(offsets)
    piece = jax.ShapeDtypeStruct((pages,) + kv_pool.shape[1:], kv_pool.dtype)
    return pl.pallas_call(
        functools.partial(pack_kernel, offsets),
        out_shape=(piece,) * count,
        in_specs=[
            pl.BlockSpec(memory_space=pltpu.SMEM),
            pl.BlockSpec(memory_space=pltpu.SMEM),
            pl.BlockSpec(memory_space=pltpu.HBM),
        ],
        out_specs=(pl.BlockSpec(memory_space=pl.ANY),) * count,
        scratch_shapes=[
            pltpu.VMEM((count, pages) + kv_pool.shape[1:], kv_pool.dtype),
            pltpu.SemaphoreType.DMA((count, pages)),
            pltpu.SemaphoreType.DMA((count, pages)),
        ],
        compiler_params=pltpu.CompilerParams(vmem_limit_bytes=LITTLE),
        cost_estimate=SMALL,
        name="pack",
    )(*(pltpu.with_memory_space_constraint(x, pltpu.HBM) for x in (moves, page_table, kv_pool)))


def place_kernel(row, guests, piece_ref, *refs):
    guest_refs, refs = refs[:guests], refs[guests:]
    held, in_sems, out_sems = refs[-3:]
    out_ref = refs[-5] if guests else refs[-4]
    rows = piece_ref.shape[1] // PARTS
    reads, writes = [], []
    for page in range(piece_ref.shape[0]):
        for part in range(PARTS):
            lines = pl.ds(part * rows, rows)
            reads.append(
                pltpu.make_async_copy(
                    piece_ref.at[page, lines], held.at[page, lines], in_sems.at[page, part]
                )
            )
            writes.append(
                pltpu.make_async_copy(
                    held.at[page, lines], out_ref.at[row + page, lines], out_sems.at[page, part]
                )
            )
            reads[-1].start()
    if guests:
        refs[-4][...] = jnp.concatenate([guest[...] for guest in guest_refs], axis=0)
    for read, write in zip(reads, writes):
        read.wait()
        write.start()
    for write in writes:
        write.wait()


def place(piece, row, total, buffer=None, guests=()):
    args = (piece, *guests)
    aliases = {}
    if buffer is not None:
        aliases = {len(args): 0}
        args += (buffer,)
    shapes = [pltpu.HBM((total,) + piece.shape[1:], piece.dtype)]
    specs = [pl.BlockSpec(memory_space=pltpu.HBM)]
    if guests:
        shapes.append(jax.ShapeDtypeStruct((len(guests), guests[0].shape[1]), guests[0].dtype))
        specs.append(pl.BlockSpec(memory_space=pltpu.VMEM))
    return pl.pallas_call(
        functools.partial(place_kernel, row, len(guests)),
        out_shape=tuple(shapes),
        in_specs=[pl.BlockSpec(memory_space=pl.ANY)]
        + [pl.BlockSpec(memory_space=pltpu.VMEM)] * len(guests)
        + [pl.BlockSpec(memory_space=pltpu.HBM)] * len(aliases),
        out_specs=tuple(specs),
        scratch_shapes=[
            pltpu.VMEM(piece.shape, piece.dtype),
            pltpu.SemaphoreType.DMA((piece.shape[0], PARTS)),
            pltpu.SemaphoreType.DMA((piece.shape[0], PARTS)),
        ],
        input_output_aliases=aliases,
        compiler_params=pltpu.CompilerParams(vmem_limit_bytes=LITTLE),
        cost_estimate=SMALL,
        name="place",
    )(*args)


def attend_kernel(moves_ref, table_ref, lengths_ref, pool_ref, query_ref, fresh_ref, *refs):
    out_ref, guest_refs = refs[0], refs[1 : 1 + REACH]
    held, asked, answered, sems = refs[1 + REACH :]
    sessions, pages = table_ref.shape
    span = pages * held.shape[2]
    reads = []
    for session in range(sessions):
        for page in range(pages):
            reads.append(
                pltpu.make_async_copy(
                    pool_ref.at[table_ref[session, page]],
                    held.at[session, page],
                    sems.at[session, page],
                )
            )
            reads[-1].start()
    for head in range(HQ):
        lanes = pl.ds(head * HD, HD)
        for step in range(STEPS):
            asked[head, pl.ds(step * sessions, sessions)] = query_ref[step, :, lanes].astype(
                jnp.float32
            )
    scale = 1.0 / jnp.sqrt(jnp.float32(HD))
    spots = lax.broadcasted_iota(jnp.int32, (1, span), 1)
    for session in range(sessions):
        for page in range(pages):
            reads[session * pages + page].wait()
        visible = spots < lengths_ref[session]
        for head in range(KVH):
            heads = pl.ds(head * GRP, GRP)
            keys = held[session, :, :, pl.ds(head * HD, HD)].reshape(span, HD)
            values = held[session, :, :, pl.ds((KVH + head) * HD, HD)].reshape(span, HD)
            query = jnp.concatenate(
                [asked[heads, step * sessions + session, :] for step in range(STEPS)], axis=0
            )

            def spread(first):
                rows = [
                    fresh_ref[step, :, pl.ds(first, HD)].astype(jnp.float32)[session : session + 1]
                    for step in range(STEPS)
                ]
                return jnp.concatenate([jnp.broadcast_to(row, (GRP, HD)) for row in rows], axis=0)

            scores = lax.dot_general(
                query.astype(jnp.bfloat16),
                keys,
                (((1,), (1,)), ((), ())),
                preferred_element_type=jnp.float32,
            )
            scores = jnp.where(visible, scores * scale, jnp.float32(-1e30))
            own = jnp.sum(query * spread(head * HD), axis=1, keepdims=True) * scale
            highest = jnp.maximum(jnp.max(scores, axis=1, keepdims=True), own)
            expo = jnp.exp(scores - highest)
            own_expo = jnp.exp(own - highest)
            denominator = jnp.sum(expo, axis=1, keepdims=True) + own_expo
            weights = (expo / denominator).astype(jnp.bfloat16)
            own_weight = (own_expo / denominator).astype(jnp.bfloat16).astype(jnp.float32)
            result = jnp.dot(weights, values, preferred_element_type=jnp.float32)
            result = result + own_weight * spread((KVH + head) * HD)
            for step in range(STEPS):
                answered[heads, step * sessions + session, :] = result[
                    step * GRP : (step + 1) * GRP
                ]
    rows = lax.broadcasted_iota(jnp.int32, (sessions, HD), 0)
    distance = jnp.zeros((sessions, HD), jnp.int32)
    for session in range(sessions):
        distance = jnp.where(rows == session, moves_ref[session], distance)
    for head in range(HQ):
        lanes = pl.ds(head * HD, HD)
        first = answered[head, pl.ds(0, sessions)]
        second = answered[head, pl.ds(sessions, sessions)]
        out_ref[0, :, lanes] = first.astype(jnp.bfloat16)
        out_ref[1, :, lanes] = jnp.where(distance > 0, 0.0, second).astype(jnp.bfloat16)
        for offset in range(1, REACH + 1):
            row = jnp.sum(jnp.where(distance == offset, second, 0.0), axis=0, keepdims=True)
            guest_refs[offset - 1][:, lanes] = row.astype(jnp.bfloat16)


def attend(kv_pool, page_table, lengths, moves, query, new_kv):
    sessions, pages = page_table.shape
    guest = jax.ShapeDtypeStruct((1, query.shape[2]), query.dtype)
    return pl.pallas_call(
        attend_kernel,
        out_shape=(jax.ShapeDtypeStruct(query.shape, query.dtype),) + (guest,) * REACH,
        in_specs=[pl.BlockSpec(memory_space=pltpu.SMEM)] * 3
        + [pl.BlockSpec(memory_space=pltpu.HBM)]
        + [pl.BlockSpec(memory_space=pltpu.VMEM)] * 2,
        out_specs=(pl.BlockSpec(memory_space=pltpu.VMEM),) * (1 + REACH),
        scratch_shapes=[
            pltpu.VMEM((sessions, pages) + kv_pool.shape[1:], kv_pool.dtype),
            pltpu.VMEM((HQ, STEPS * sessions, HD), jnp.float32),
            pltpu.VMEM((HQ, STEPS * sessions, HD), jnp.float32),
            pltpu.SemaphoreType.DMA((sessions, pages)),
        ],
        compiler_params=pltpu.CompilerParams(vmem_limit_bytes=16 << 20),
        cost_estimate=SMALL,
        name="attend",
    )(
        *(
            pltpu.with_memory_space_constraint(x, pltpu.HBM)
            for x in (moves, page_table, lengths, kv_pool, query, new_kv)
        )
    )


def body(kv_pool, page_table, lengths, query, new_kv, moves):
    count = lax.axis_size("inst")
    sessions, pages = page_table.shape
    total = REACH * pages
    near, far = pack((1, 3), moves, page_table, kv_pool)
    near, far, table, query, new_kv = lax.optimization_barrier(
        (near, far, page_table, query, new_kv)
    )
    (middle,) = pack((2,), moves, table, kv_pool)
    attended, *leaving = attend(kv_pool, table, lengths, moves, query, new_kv)
    attended, middle, *leaving = lax.optimization_barrier((attended, middle, *leaving))
    if count % 4 == 0:
        hops = relay_pairs(count)
    else:
        hops = (shift_pairs(count, 1),)
    near = send(near, hops[0])
    far = send(far, shift_pairs(count, 3))
    middle = send(middle, shift_pairs(count, 2))
    guests = [
        send(leaving[offset - 1], shift_pairs(count, offset))
        for offset in range(1, REACH + 1)
    ]
    for hop in hops[1:]:
        near = send(near, hop)
    (moved,) = place(far, 2 * pages, total)
    (moved,) = place(middle, pages, total, moved)
    moved, near, *guests = lax.optimization_barrier((moved, near, *guests))
    moved, guest_attended = place(near, 0, total, moved, guests)
    return attended, guest_attended, moved


def solution(mesh):
    return jax.shard_map(
        body,
        mesh=mesh,
        in_specs=(
            P(("group", "inst"), None, None),
            P(("group", "inst"), None),
            P(("group", "inst")),
            P(None, ("group", "inst"), None),
            P(None, ("group", "inst"), None),
            P(("group", "inst")),
        ),
        out_specs=(
            P(None, ("group", "inst"), None),
            P(("group", "inst"), None),
            P(("group", "inst"), None, None),
        ),
        check_vma=False,
    )
```

time: 89.2 us -> 83 us (0.930)
  waiting for transfers between devices: 29 us -> 42.4 us
  starting transfers between devices: 25.3 us -> 16 us
  Pallas kernels: 30 us -> 23.6 us
  local copies, waits for them, and re-layouts: 2.44 us -> 0 us
    ppermute x7, waiting for transfers between devices: 29 us -> 42.4 us  [send(): return lax.ppermute(value, 'inst', pairs)]
    ppermute x7, starting transfers between devices: 25.3 us -> 16 us  [send(): return lax.ppermute(value, 'inst', pairs)]
    pallas_call x4, Pallas kernels: 24.5 us -> 18.8 us  [the longest x1 14 us: attend(): pl.pallas_call(attend_kernel, out_shape=(jax.ShapeDtypeStruct(query.shape...]
    unnamed x15 -> x0, local copies, waits for them, and re-layouts: 1.4 us -> none
    reshape x4 -> x0, local copies, waits for them, and re-layouts: 0.9 us -> none  [the longest x1 0.69 us: body(): attended = full.reshape(STEPS, sessions, HQ * HD)]
  transfers between devices with their start and end apart: 7 -> 7, of which waited for: 4 -> 2; matrix products, arithmetic and copies ran while one was open for 2% -> 0% of each run, Pallas kernels for 27% -> 23%
where the time goes in v3:
time: 83 us; the launch traced here: 82.8 us
  waiting for transfers between devices  42.4 us (51%)
  Pallas kernels  23.6 us (28%)
  starting transfers between devices  16 us (19%)
    ppermute x7, waiting for transfers between devices, send(): return lax.ppermute(value, 'inst', pairs)  42.4 us
    ppermute x7, starting transfers between devices, send(): return lax.ppermute(value, 'inst', pairs)  16 us
    pallas_call x1, Pallas kernels, attend(): pl.pallas_call(attend_kernel, out_shape=(jax.ShapeDtypeStruct(query.shape...  14 us
    pallas_call x2, Pallas kernels, pack(): pl.pallas_call(functools.partial(pack_kernel, offsets), out_shape=(piece,...  4.85 us
    pallas_call x3, Pallas kernels, place(): pl.pallas_call(functools.partial(place_kernel, row, len(guests)), out_sha...  4.76 us
  transfers between devices with their start and end apart: 7, of which 2 were waited for; matrix products, arithmetic and copies ran while one was open for 0% of the time, Pallas kernels for 23%

profile of v3, /device:TPU:0, one launch (start us, length us, event | category | flops | bytes accessed | tf_op | source)
XLA Modules:
  0.0 82.8 jit_solution(6011711024195923752)
XLA Ops:
  0.6 2.7 %pack.2 = (bf16[3,128,2048]{2,1,0:T(8,128)(2,1)S(1)}, bf16[3,128,2048]{2,1,0:T(8,128)(2,1)S(1)}) custom-call(s32[4]{0:T(128)} %moves_ref.5, s32[4,3]{1,0:T(4,128)} %table_ref.3, bf16[12,128,2048]{2,1,0:T(8,128)(2,1)} %pool_ref.5), custom_call_target="tpu_custom_call" | custom-call | tf_op jit(solution)/shard_map/pack/pallas_call | solution.py:64
  3.3 0.5 collective-permute-start.2
  3.8 2.0 %collective-permute-start.1 = (bf16[3,128,2048]{2,1,0:T(8,128)(2,1)S(1)}, bf16[3,128,2048]{2,1,0:T(8,128)(2,1)S(1)}, u32[]{:S(2)}, u32[]{:S(2)}) collective-permute-start(bf16[3,128,2048]{2,1,0:T(8,128)(2,1)S(1)} %get-tuple-element.37), channel_id=1, source_target_pairs={{0,3},{1,4},{2,5},{3,6},{4,7},{5,8},{6,9},{7,10},{8,11},{9,12},{10... | collective-permute-start | bytes 4718600 | tf_op jit(solution)/shard_map/ppermute | solution.py:22
  5.8 2.2 %pack.3 = bf16[3,128,2048]{2,1,0:T(8,128)(2,1)S(1)} custom-call(s32[4]{0:T(128)} %moves_ref.5, s32[4,3]{1,0:T(4,128)} %table_ref.3, bf16[12,128,2048]{2,1,0:T(8,128)(2,1)} %pool_ref.5), custom_call_target="tpu_custom_call" | custom-call | tf_op jit(solution)/shard_map/pack/pallas_call | solution.py:64
  8.0 14.0 %attend.1 = (bf16[2,4,8192]{2,1,0:T(4,128)(2,1)}, bf16[1,8192]{1,0:T(2,128)(2,1)S(1)}, bf16[1,8192]{1,0:T(2,128)(2,1)S(1)}, bf16[1,8192]{1,0:T(2,128)(2,1)S(1)}) custom-call(s32[4]{0:T(128)} %moves_ref.5, s32[4,3]{1,0:T(4,128)} %table_ref.3, s32[4]{0:T(128)} %lengths_ref.1, bf16[12,128,2048]{2,1,0:T(8,128)(2,1)} %pool_ref.5, bf16[2,4,8192]{2,1,0:T(4,128)(2,1)} %query_ref, ...), custom_call_target="tpu_custom_call" | custom-call | tf_op jit(solution)/shard_map/attend/pallas_call | solution.py:224
  22.0 3.3 %collective-permute-start = (bf16[3,128,2048]{2,1,0:T(8,128)(2,1)S(1)}, bf16[3,128,2048]{2,1,0:T(8,128)(2,1)S(1)}, u32[]{:S(2)}, u32[]{:S(2)}) collective-permute-start(bf16[3,128,2048]{2,1,0:T(8,128)(2,1)S(1)} %pack.3), channel_id=1, source_target_pairs={{0,2},{1,3},{2,4},{3,5},{4,6},{5,7},{6,8},{7,9},{8,10},{9,11},{10,... | collective-permute-start | bytes 4718600 | tf_op jit(solution)/shard_map/ppermute | solution.py:22
  25.4 10.0 %collective-permute-done.2 = bf16[3,128,2048]{2,1,0:T(8,128)(2,1)S(1)} collective-permute-done((bf16[3,128,2048]{2,1,0:T(8,128)(2,1)S(1)}, bf16[3,128,2048]{2,1,0:T(8,128)(2,1)S(1)}, u32[]{:S(2)}, u32[]{:S(2)}) %collective-permute-start.2) | collective-permute-done | bytes 1572896 | tf_op jit(solution)/shard_map/ppermute | solution.py:22
  35.3 6.9 %collective-permute-start.3 = (bf16[3,128,2048]{2,1,0:T(8,128)(2,1)S(1)}, bf16[3,128,2048]{2,1,0:T(8,128)(2,1)S(1)}, u32[]{:S(2)}, u32[]{:S(2)}) collective-permute-start(bf16[3,128,2048]{2,1,0:T(8,128)(2,1)S(1)} %collective-permute-done.2), channel_id=1, source_target_pairs={{0,4},{1,1},{2,2},{3,3},{4,8},{5,5},{6,6},{7,7},{8,12},{9,9},{10,1... | collective-permute-start | bytes 4718600 | tf_op jit(solution)/shard_map/ppermute | solution.py:22
  42.2 0.1 collective-permute-start.4
  42.3 1.6 %collective-permute-start.5 = (bf16[1,8192]{1,0:T(2,128)(2,1)S(1)}, bf16[1,8192]{1,0:T(2,128)(2,1)S(1)}, u32[]{:S(2)}, u32[]{:S(2)}) collective-permute-start(bf16[1,8192]{1,0:T(2,128)(2,1)S(1)} %get-tuple-element.40), channel_id=1, source_target_pairs={{0,2},{1,3},{2,4},{3,5},{4,6},{5,7},{6,8},{7,9},{8,10},{9,11},{10,... | collective-permute-start | bytes 49160 | tf_op jit(solution)/shard_map/ppermute | solution.py:22
  43.9 0.0 collective-permute-done.1.piece_ref
  43.9 1.7 %collective-permute-start.6 = (bf16[1,8192]{1,0:T(2,128)(2,1)S(1)}, bf16[1,8192]{1,0:T(2,128)(2,1)S(1)}, u32[]{:S(2)}, u32[]{:S(2)}) collective-permute-start(bf16[1,8192]{1,0:T(2,128)(2,1)S(1)} %get-tuple-element.41), channel_id=1, source_target_pairs={{0,3},{1,4},{2,5},{3,6},{4,7},{5,8},{6,9},{7,10},{8,11},{9,12},{10... | collective-permute-start | bytes 49160 | tf_op jit(solution)/shard_map/ppermute | solution.py:22
  45.5 1.3 %place.3.refs_0_ = bf16[9,128,2048]{2,1,0:T(8,128)(2,1)} custom-call(bf16[3,128,2048]{2,1,0:T(8,128)(2,1)S(1)} %collective-permute-done.1.piece_ref), custom_call_target="tpu_custom_call" | custom-call | tf_op jit(solution)/shard_map/place/pallas_call | solution.py:124
  46.9 32.4 %collective-permute-done.piece_ref = bf16[3,128,2048]{2,1,0:T(8,128)(2,1)S(1)} collective-permute-done((bf16[3,128,2048]{2,1,0:T(8,128)(2,1)S(1)}, bf16[3,128,2048]{2,1,0:T(8,128)(2,1)S(1)}, u32[]{:S(2)}, u32[]{:S(2)}) %collective-permute-start) | collective-permute-done | bytes 1572896 | tf_op jit(solution)/shard_map/ppermute | solution.py:22
  79.3 1.3 %place.4.refs_3_ = bf16[9,128,2048]{2,1,0:T(8,128)(2,1)} custom-call(bf16[3,128,2048]{2,1,0:T(8,128)(2,1)S(1)} %collective-permute-done.piece_ref, bf16[9,128,2048]{2,1,0:T(8,128)(2,1)} %place.3.refs_0_), custom_call_target="tpu_custom_call", output_to_operand_aliasing={{}: (1, {})} | custom-call | tf_op jit(solution)/shard_map/place/pallas_call | solution.py:124
  80.7 0.0 collective-permute-done.4.refs_0_
  80.7 0.0 collective-permute-done.5.refs_1_
  80.7 0.0 collective-permute-done.6.refs_2_
  80.7 0.0 collective-permute-done.3.piece_ref
  80.7 2.1 %place.5 = (bf16[9,128,2048]{2,1,0:T(8,128)(2,1)}, bf16[3,8192]{1,0:T(4,128)(2,1)}) custom-call(bf16[3,128,2048]{2,1,0:T(8,128)(2,1)S(1)} %collective-permute-done.3.piece_ref, bf16[1,8192]{1,0:T(2,128)(2,1)S(1)} %collective-permute-done.4.refs_0_, bf16[1,8192]{1,0:T(2,128)(2,1)S(1)} %collective-permute-done.5.refs_1_, ...), custom_call_target="tpu_custom_call", output_to_operand_aliasing={{0}: (4, {})} | custom-call | tf_op jit(solution)/shard_map/place/pallas_call | solution.py:124
Async XLA Ops:
  3.3 32.0 %collective-permute-start.2 = (bf16[3,128,2048]{2,1,0:T(8,128)(2,1)S(1)}, bf16[3,128,2048]{2,1,0:T(8,128)(2,1)S(1)}, u32[]{:S(2)}, u32[]{:S(2)}) collective-permute-start(bf16[3,128,2048]{2,1,0:T(8,128)(2,1)S(1)} %get-tuple-element.38), channel_id=1, source_target_pairs={{0,1},{1,2},{2,3},{3,0},{4,5},{5,6},{6,7},{7,4},{8,9},{9,10},{10,1... | collective-permute-start | bytes 4718600 | tf_op jit(solution)/shard_map/ppermute | solution.py:22
  3.8 40.0 %collective-permute-start.1 = (bf16[3,128,2048]{2,1,0:T(8,128)(2,1)S(1)}, bf16[3,128,2048]{2,1,0:T(8,128)(2,1)S(1)}, u32[]{:S(2)}, u32[]{:S(2)}) collective-permute-start(bf16[3,128,2048]{2,1,0:T(8,128)(2,1)S(1)} %get-tuple-element.37), channel_id=1, source_target_pairs={{0,3},{1,4},{2,5},{3,6},{4,7},{5,8},{6,9},{7,10},{8,11},{9,12},{10... | collective-permute-start | bytes 4718600 | tf_op jit(solution)/shard_map/ppermute | solution.py:22
  22.0 57.3 %collective-permute-start = (bf16[3,128,2048]{2,1,0:T(8,128)(2,1)S(1)}, bf16[3,128,2048]{2,1,0:T(8,128)(2,1)S(1)}, u32[]{:S(2)}, u32[]{:S(2)}) collective-permute-start(bf16[3,128,2048]{2,1,0:T(8,128)(2,1)S(1)} %pack.3), channel_id=1, source_target_pairs={{0,2},{1,3},{2,4},{3,5},{4,6},{5,7},{6,8},{7,9},{8,10},{9,11},{10,... | collective-permute-start | bytes 4718600 | tf_op jit(solution)/shard_map/ppermute | solution.py:22
  35.3 45.4 %collective-permute-start.3 = (bf16[3,128,2048]{2,1,0:T(8,128)(2,1)S(1)}, bf16[3,128,2048]{2,1,0:T(8,128)(2,1)S(1)}, u32[]{:S(2)}, u32[]{:S(2)}) collective-permute-start(bf16[3,128,2048]{2,1,0:T(8,128)(2,1)S(1)} %collective-permute-done.2), channel_id=1, source_target_pairs={{0,4},{1,1},{2,2},{3,3},{4,8},{5,5},{6,6},{7,7},{8,12},{9,9},{10,1... | collective-permute-start | bytes 4718600 | tf_op jit(solution)/shard_map/ppermute | solution.py:22
  42.2 38.5 %collective-permute-start.4 = (bf16[1,8192]{1,0:T(2,128)(2,1)S(1)}, bf16[1,8192]{1,0:T(2,128)(2,1)S(1)}, u32[]{:S(2)}, u32[]{:S(2)}) collective-permute-start(bf16[1,8192]{1,0:T(2,128)(2,1)S(1)} %get-tuple-element.39), channel_id=1, source_target_pairs={{0,1},{1,2},{2,3},{3,4},{4,5},{5,6},{6,7},{7,8},{8,9},{9,10},{10,1... | collective-permute-start | bytes 49160 | tf_op jit(solution)/shard_map/ppermute | solution.py:22
  42.3 38.4 %collective-permute-start.5 = (bf16[1,8192]{1,0:T(2,128)(2,1)S(1)}, bf16[1,8192]{1,0:T(2,128)(2,1)S(1)}, u32[]{:S(2)}, u32[]{:S(2)}) collective-permute-start(bf16[1,8192]{1,0:T(2,128)(2,1)S(1)} %get-tuple-element.40), channel_id=1, source_target_pairs={{0,2},{1,3},{2,4},{3,5},{4,6},{5,7},{6,8},{7,9},{8,10},{9,11},{10,... | collective-permute-start | bytes 49160 | tf_op jit(solution)/shard_map/ppermute | solution.py:22
  43.9 36.9 %collective-permute-start.6 = (bf16[1,8192]{1,0:T(2,128)(2,1)S(1)}, bf16[1,8192]{1,0:T(2,128)(2,1)S(1)}, u32[]{:S(2)}, u32[]{:S(2)}) collective-permute-start(bf16[1,8192]{1,0:T(2,128)(2,1)S(1)} %get-tuple-element.41), channel_id=1, source_target_pairs={{0,3},{1,4},{2,5},{3,6},{4,7},{5,8},{6,9},{7,10},{8,11},{9,12},{10... | collective-permute-start | bytes 49160 | tf_op jit(solution)/shard_map/ppermute | solution.py:22

commit v4 on v3

--- a/solution.py
+++ b/solution.py
@@ -14,8 +14,7 @@
 GRP = 8
 STEPS = 2
 SMALL = pl.CostEstimate(flops=0, bytes_accessed=0, transcendentals=0)
-LITTLE = 5 << 20
-PARTS = 2
+LITTLE = 1 << 20
 
 
 def send(value, pairs):
@@ -33,106 +32,83 @@
 
 
 def pack_kernel(offsets, moves_ref, table_ref, pool_ref, *refs):
-    outs, held, in_sems, out_sems = refs[: len(offsets)], *refs[-3:]
-    spots, reads, writes = [], [], []
+    outs, sems = refs[:-1], refs[-1]
+    copies = []
     for at, offset in enumerate(offsets):
         mover = jnp.int32(0)
         for session in range(1, table_ref.shape[0]):
             mover = jnp.where(moves_ref[session] == offset, jnp.int32(session), mover)
         for page in range(table_ref.shape[1]):
-            spots.append((at, page))
-            reads.append(
+            copies.append(
                 pltpu.make_async_copy(
-                    pool_ref.at[table_ref[mover, page]], held.at[at, page], in_sems.at[at, page]
+                    pool_ref.at[table_ref[mover, page]], outs[at].at[page], sems.at[at, page]
                 )
             )
-            reads[-1].start()
-    for (at, page), read in zip(spots, reads):
-        read.wait()
-        writes.append(
-            pltpu.make_async_copy(held.at[at, page], outs[at].at[page], out_sems.at[at, page])
-        )
-        writes[-1].start()
-    for write in writes:
-        write.wait()
+            copies[-1].start()
+    for copy in copies:
+        copy.wait()
 
 
 def pack(offsets, moves, page_table, kv_pool):
     pages = page_table.shape[1]
-    count = len(offsets)
     piece = jax.ShapeDtypeStruct((pages,) + kv_pool.shape[1:], kv_pool.dtype)
     return pl.pallas_call(
         functools.partial(pack_kernel, offsets),
-        out_shape=(piece,) * count,
+        out_shape=(piece,) * len(offsets),
         in_specs=[
             pl.BlockSpec(memory_space=pltpu.SMEM),
             pl.BlockSpec(memory_space=pltpu.SMEM),
             pl.BlockSpec(memory_space=pltpu.HBM),
         ],
-        out_specs=(pl.BlockSpec(memory_space=pl.ANY),) * count,
-        scratch_shapes=[
-            pltpu.VMEM((count, pages) + kv_pool.shape[1:], kv_pool.dtype),
-            pltpu.SemaphoreType.DMA((count, pages)),
-            pltpu.SemaphoreType.DMA((count, pages)),
-        ],
+        out_specs=(pl.BlockSpec(memory_space=pl.ANY),) * len(offsets),
+        scratch_shapes=[pltpu.SemaphoreType.DMA((len(offsets), pages))],
         compiler_params=pltpu.CompilerParams(vmem_limit_bytes=LITTLE),
         cost_estimate=SMALL,
         name="pack",
     )(*(pltpu.with_memory_space_constraint(x, pltpu.HBM) for x in (moves, page_table, kv_pool)))
 
 
-def place_kernel(row, guests, piece_ref, *refs):
+def place_kernel(rows, guests, *refs):
+    pieces, refs = refs[: len(rows)], refs[len(rows) :]
     guest_refs, refs = refs[:guests], refs[guests:]
-    held, in_sems, out_sems = refs[-3:]
-    out_ref = refs[-5] if guests else refs[-4]
-    rows = piece_ref.shape[1] // PARTS
-    reads, writes = [], []
-    for page in range(piece_ref.shape[0]):
-        for part in range(PARTS):
-            lines = pl.ds(part * rows, rows)
-            reads.append(
-                pltpu.make_async_copy(
-                    piece_ref.at[page, lines], held.at[page, lines], in_sems.at[page, part]
-                )
-            )
-            writes.append(
-                pltpu.make_async_copy(
-                    held.at[page, lines], out_ref.at[row + page, lines], out_sems.at[page, part]
-                )
-            )
-            reads[-1].start()
     if guests:
-        refs[-4][...] = jnp.concatenate([guest[...] for guest in guest_refs], axis=0)
-    for read, write in zip(reads, writes):
-        read.wait()
-        write.start()
-    for write in writes:
-        write.wait()
-
-
-def place(piece, row, total, buffer=None, guests=()):
-    args = (piece, *guests)
+        out_ref, guest_out_ref, held, sem, guest_sem = refs[-5:]
+    else:
+        out_ref, sem = refs[-2:]
+    copies = []
+    for at, (row, piece) in enumerate(zip(rows, pieces)):
+        copies.append(
+            pltpu.make_async_copy(piece, out_ref.at[pl.ds(row, piece.shape[0])], sem.at[at])
+        )
+        copies[-1].start()
+    if guests:
+        held[...] = jnp.concatenate([guest[...] for guest in guest_refs], axis=0)
+        copies.append(pltpu.make_async_copy(held, guest_out_ref, guest_sem))
+        copies[-1].start()
+    for copy in copies:
+        copy.wait()
+
+
+def place(pieces, rows, total, buffer=None, guests=()):
+    args = (*pieces, *guests)
     aliases = {}
     if buffer is not None:
         aliases = {len(args): 0}
         args += (buffer,)
-    shapes = [pltpu.HBM((total,) + piece.shape[1:], piece.dtype)]
-    specs = [pl.BlockSpec(memory_space=pltpu.HBM)]
+    shapes = [pltpu.HBM((total,) + pieces[0].shape[1:], pieces[0].dtype)]
+    scratch = [pltpu.SemaphoreType.DMA((len(pieces),))]
     if guests:
-        shapes.append(jax.ShapeDtypeStruct((len(guests), guests[0].shape[1]), guests[0].dtype))
-        specs.append(pl.BlockSpec(memory_space=pltpu.VMEM))
+        guest = (len(guests), guests[0].shape[1])
+        shapes.append(pltpu.HBM(guest, guests[0].dtype))
+        scratch = [pltpu.VMEM(guest, guests[0].dtype)] + scratch + [pltpu.SemaphoreType.DMA]
     return pl.pallas_call(
-        functools.partial(place_kernel, row, len(guests)),
+        functools.partial(place_kernel, rows, len(guests)),
         out_shape=tuple(shapes),
-        in_specs=[pl.BlockSpec(memory_space=pl.ANY)]
+        in_specs=[pl.BlockSpec(memory_space=pl.ANY)] * len(pieces)
         + [pl.BlockSpec(memory_space=pltpu.VMEM)] * len(guests)
         + [pl.BlockSpec(memory_space=pltpu.HBM)] * len(aliases),
-        out_specs=tuple(specs),
-        scratch_shapes=[
-            pltpu.VMEM(piece.shape, piece.dtype),
-            pltpu.SemaphoreType.DMA((piece.shape[0], PARTS)),
-            pltpu.SemaphoreType.DMA((piece.shape[0], PARTS)),
-        ],
+        out_specs=(pl.BlockSpec(memory_space=pltpu.HBM),) * len(shapes),
+        scratch_shapes=scratch,
         input_output_aliases=aliases,
         compiler_params=pltpu.CompilerParams(vmem_limit_bytes=LITTLE),
         cost_estimate=SMALL,
@@ -267,12 +243,11 @@
         send(leaving[offset - 1], shift_pairs(count, offset))
         for offset in range(1, REACH + 1)
     ]
+    (moved,) = place((far,), (2 * pages,), total)
+    near, moved = lax.optimization_barrier((near, moved))
     for hop in hops[1:]:
         near = send(near, hop)
-    (moved,) = place(far, 2 * pages, total)
-    (moved,) = place(middle, pages, total, moved)
-    moved, near, *guests = lax.optimization_barrier((moved, near, *guests))
-    moved, guest_attended = place(near, 0, total, moved, guests)
+    moved, guest_attended = place((middle, near), (pages, 0), total, moved, guests)
     return attended, guest_attended, moved
 
 

time: 83 us -> 80.8 us (0.973)
  starting transfers between devices: 16 us -> 12.8 us
  waiting for transfers between devices: 42.4 us -> 45.5 us
  Pallas kernels: 23.6 us -> 21.6 us
    ppermute x7, starting transfers between devices: 16 us -> 12.8 us  [send(): return lax.ppermute(value, 'inst', pairs)]
    ppermute x7, waiting for transfers between devices: 42.4 us -> 45.5 us  [send(): return lax.ppermute(value, 'inst', pairs)]
    pallas_call x3 -> x2, Pallas kernels: 4.76 us -> 2.85 us  [place(): pl.pallas_call(functools.partial(place_kernel, rows, len(guests)), out_sh...]
  transfers between devices with their start and end apart: 7 -> 7, of which waited for: 2 -> 3; matrix products, arithmetic and copies ran while one was open for 0% -> 0% of each run, Pallas kernels for 23% -> 21%
where the time goes in v4:
time: 80.8 us; the launch traced here: 80.5 us
  waiting for transfers between devices  45.5 us (56%)
  Pallas kernels  21.6 us (27%)
  starting transfers between devices  12.8 us (16%)
    ppermute x7, waiting for transfers between devices, send(): return lax.ppermute(value, 'inst', pairs)  45.5 us
    pallas_call x1, Pallas kernels, attend(): pl.pallas_call(attend_kernel, out_shape=(jax.ShapeDtypeStruct(query.shape...  14 us
    ppermute x7, starting transfers between devices, send(): return lax.ppermute(value, 'inst', pairs)  12.8 us
    pallas_call x2, Pallas kernels, pack(): pl.pallas_call(functools.partial(pack_kernel, offsets), out_shape=(piece,...  4.68 us
    pallas_call x2, Pallas kernels, place(): pl.pallas_call(functools.partial(place_kernel, rows, len(guests)), out_sh...  2.85 us
  transfers between devices with their start and end apart: 7, of which 3 were waited for; matrix products, arithmetic and copies ran while one was open for 0% of the time, Pallas kernels for 21%

profile of v4, /device:TPU:0, one launch (start us, length us, event | category | flops | bytes accessed | tf_op | source)
XLA Modules:
  0.0 80.5 jit_solution(6162125619669058350)
XLA Ops:
  0.6 2.6 %pack.2 = (bf16[3,128,2048]{2,1,0:T(8,128)(2,1)S(1)}, bf16[3,128,2048]{2,1,0:T(8,128)(2,1)S(1)}) custom-call(s32[4]{0:T(128)} %moves_ref.5, s32[4,3]{1,0:T(4,128)} %table_ref.3, bf16[12,128,2048]{2,1,0:T(8,128)(2,1)} %pool_ref.5), custom_call_target="tpu_custom_call" | custom-call | tf_op jit(solution)/shard_map/pack/pallas_call | solution.py:55
  3.2 2.4 %collective-permute-start.2 = (bf16[3,128,2048]{2,1,0:T(8,128)(2,1)S(1)}, bf16[3,128,2048]{2,1,0:T(8,128)(2,1)S(1)}, u32[]{:S(2)}, u32[]{:S(2)}) collective-permute-start(bf16[3,128,2048]{2,1,0:T(8,128)(2,1)S(1)} %get-tuple-element.35), channel_id=1, source_target_pairs={{0,3},{1,4},{2,5},{3,6},{4,7},{5,8},{6,9},{7,10},{8,11},{9,12},{10... | collective-permute-start | bytes 4718600 | tf_op jit(solution)/shard_map/ppermute | solution.py:21
  5.7 0.8 collective-permute-start.1
  6.4 2.1 %pack.3 = bf16[3,128,2048]{2,1,0:T(8,128)(2,1)S(1)} custom-call(s32[4]{0:T(128)} %moves_ref.5, s32[4,3]{1,0:T(4,128)} %table_ref.3, bf16[12,128,2048]{2,1,0:T(8,128)(2,1)} %pool_ref.5), custom_call_target="tpu_custom_call" | custom-call | tf_op jit(solution)/shard_map/pack/pallas_call | solution.py:55
  8.5 14.0 %attend.1 = (bf16[2,4,8192]{2,1,0:T(4,128)(2,1)}, bf16[1,8192]{1,0:T(2,128)(2,1)S(1)}, bf16[1,8192]{1,0:T(2,128)(2,1)S(1)}, bf16[1,8192]{1,0:T(2,128)(2,1)S(1)}) custom-call(s32[4]{0:T(128)} %moves_ref.5, s32[4,3]{1,0:T(4,128)} %table_ref.3, s32[4]{0:T(128)} %lengths_ref.1, bf16[12,128,2048]{2,1,0:T(8,128)(2,1)} %pool_ref.5, bf16[2,4,8192]{2,1,0:T(4,128)(2,1)} %query_ref, ...), custom_call_target="tpu_custom_call" | custom-call | tf_op jit(solution)/shard_map/attend/pallas_call | solution.py:200
  22.6 1.5 %collective-permute-start = (bf16[3,128,2048]{2,1,0:T(8,128)(2,1)S(1)}, bf16[3,128,2048]{2,1,0:T(8,128)(2,1)S(1)}, u32[]{:S(2)}, u32[]{:S(2)}) collective-permute-start(bf16[3,128,2048]{2,1,0:T(8,128)(2,1)S(1)} %pack.3), channel_id=1, source_target_pairs={{0,2},{1,3},{2,4},{3,5},{4,6},{5,7},{6,8},{7,9},{8,10},{9,11},{10,... | collective-permute-start | bytes 4718600 | tf_op jit(solution)/shard_map/ppermute | solution.py:21
  24.1 15.4 %collective-permute-done.2.refs_0_ = bf16[3,128,2048]{2,1,0:T(8,128)(2,1)S(1)} collective-permute-done((bf16[3,128,2048]{2,1,0:T(8,128)(2,1)S(1)}, bf16[3,128,2048]{2,1,0:T(8,128)(2,1)S(1)}, u32[]{:S(2)}, u32[]{:S(2)}) %collective-permute-start.2) | collective-permute-done | bytes 1572896 | tf_op jit(solution)/shard_map/ppermute | solution.py:21
  39.5 1.1 %place.2.refs_5_ = bf16[9,128,2048]{2,1,0:T(8,128)(2,1)} custom-call(bf16[3,128,2048]{2,1,0:T(8,128)(2,1)S(1)} %collective-permute-done.2.refs_0_), custom_call_target="tpu_custom_call" | custom-call | tf_op jit(solution)/shard_map/place/pallas_call | solution.py:104
  40.6 0.0 collective-permute-done.1
  40.6 5.2 %collective-permute-start.3 = (bf16[3,128,2048]{2,1,0:T(8,128)(2,1)S(1)}, bf16[3,128,2048]{2,1,0:T(8,128)(2,1)S(1)}, u32[]{:S(2)}, u32[]{:S(2)}) collective-permute-start(bf16[3,128,2048]{2,1,0:T(8,128)(2,1)S(1)} %collective-permute-done.1), channel_id=1, source_target_pairs={{0,4},{1,1},{2,2},{3,3},{4,8},{5,5},{6,6},{7,7},{8,12},{9,9},{10,1... | collective-permute-start | bytes 4718600 | tf_op jit(solution)/shard_map/ppermute | solution.py:21
  45.9 0.3 collective-permute-start.4
  46.2 0.3 collective-permute-start.5
  46.5 2.2 %collective-permute-start.6 = (bf16[1,8192]{1,0:T(2,128)(2,1)S(1)}, bf16[1,8192]{1,0:T(2,128)(2,1)S(1)}, u32[]{:S(2)}, u32[]{:S(2)}) collective-permute-start(bf16[1,8192]{1,0:T(2,128)(2,1)S(1)} %get-tuple-element.39), channel_id=1, source_target_pairs={{0,3},{1,4},{2,5},{3,6},{4,7},{5,8},{6,9},{7,10},{8,11},{9,12},{10... | collective-permute-start | bytes 49160 | tf_op jit(solution)/shard_map/ppermute | solution.py:21
  48.7 29.5 %collective-permute-done.4.refs_2_ = bf16[1,8192]{1,0:T(2,128)(2,1)S(1)} collective-permute-done((bf16[1,8192]{1,0:T(2,128)(2,1)S(1)}, bf16[1,8192]{1,0:T(2,128)(2,1)S(1)}, u32[]{:S(2)}, u32[]{:S(2)}) %collective-permute-start.4) | collective-permute-done | bytes 16416 | tf_op jit(solution)/shard_map/ppermute | solution.py:21
  78.3 0.5 collective-permute-done.5.refs_3_
  78.8 0.0 collective-permute-done.6.refs_4_
  78.8 0.0 collective-permute-done.refs_0_
  78.8 0.0 collective-permute-done.3.refs_1_
  78.8 1.7 %place.3 = (bf16[9,128,2048]{2,1,0:T(8,128)(2,1)}, bf16[3,8192]{1,0:T(4,128)(2,1)}) custom-call(bf16[3,128,2048]{2,1,0:T(8,128)(2,1)S(1)} %collective-permute-done.refs_0_, bf16[3,128,2048]{2,1,0:T(8,128)(2,1)S(1)} %collective-permute-done.3.refs_1_, bf16[1,8192]{1,0:T(2,128)(2,1)S(1)} %collective-permute-done.4.refs_2_, ...), custom_call_target="tpu_custom_call", output_to_operand_aliasing={{0}: (5, {})} | custom-call | tf_op jit(solution)/shard_map/place/pallas_call | solution.py:104
Async XLA Ops:
  3.2 36.2 %collective-permute-start.2 = (bf16[3,128,2048]{2,1,0:T(8,128)(2,1)S(1)}, bf16[3,128,2048]{2,1,0:T(8,128)(2,1)S(1)}, u32[]{:S(2)}, u32[]{:S(2)}) collective-permute-start(bf16[3,128,2048]{2,1,0:T(8,128)(2,1)S(1)} %get-tuple-element.35), channel_id=1, source_target_pairs={{0,3},{1,4},{2,5},{3,6},{4,7},{5,8},{6,9},{7,10},{8,11},{9,12},{10... | collective-permute-start | bytes 4718600 | tf_op jit(solution)/shard_map/ppermute | solution.py:21
  5.7 35.0 %collective-permute-start.1 = (bf16[3,128,2048]{2,1,0:T(8,128)(2,1)S(1)}, bf16[3,128,2048]{2,1,0:T(8,128)(2,1)S(1)}, u32[]{:S(2)}, u32[]{:S(2)}) collective-permute-start(bf16[3,128,2048]{2,1,0:T(8,128)(2,1)S(1)} %get-tuple-element.34), channel_id=1, source_target_pairs={{0,1},{1,2},{2,3},{3,0},{4,5},{5,6},{6,7},{7,4},{8,9},{9,10},{10,1... | collective-permute-start | bytes 4718600 | tf_op jit(solution)/shard_map/ppermute | solution.py:21
  22.6 56.3 %collective-permute-start = (bf16[3,128,2048]{2,1,0:T(8,128)(2,1)S(1)}, bf16[3,128,2048]{2,1,0:T(8,128)(2,1)S(1)}, u32[]{:S(2)}, u32[]{:S(2)}) collective-permute-start(bf16[3,128,2048]{2,1,0:T(8,128)(2,1)S(1)} %pack.3), channel_id=1, source_target_pairs={{0,2},{1,3},{2,4},{3,5},{4,6},{5,7},{6,8},{7,9},{8,10},{9,11},{10,... | collective-permute-start | bytes 4718600 | tf_op jit(solution)/shard_map/ppermute | solution.py:21
  40.6 38.2 %collective-permute-start.3 = (bf16[3,128,2048]{2,1,0:T(8,128)(2,1)S(1)}, bf16[3,128,2048]{2,1,0:T(8,128)(2,1)S(1)}, u32[]{:S(2)}, u32[]{:S(2)}) collective-permute-start(bf16[3,128,2048]{2,1,0:T(8,128)(2,1)S(1)} %collective-permute-done.1), channel_id=1, source_target_pairs={{0,4},{1,1},{2,2},{3,3},{4,8},{5,5},{6,6},{7,7},{8,12},{9,9},{10,1... | collective-permute-start | bytes 4718600 | tf_op jit(solution)/shard_map/ppermute | solution.py:21
  45.9 32.4 %collective-permute-start.4 = (bf16[1,8192]{1,0:T(2,128)(2,1)S(1)}, bf16[1,8192]{1,0:T(2,128)(2,1)S(1)}, u32[]{:S(2)}, u32[]{:S(2)}) collective-permute-start(bf16[1,8192]{1,0:T(2,128)(2,1)S(1)} %get-tuple-element.37), channel_id=1, source_target_pairs={{0,1},{1,2},{2,3},{3,4},{4,5},{5,6},{6,7},{7,8},{8,9},{9,10},{10,1... | collective-permute-start | bytes 49160 | tf_op jit(solution)/shard_map/ppermute | solution.py:21
  46.2 32.6 %collective-permute-start.5 = (bf16[1,8192]{1,0:T(2,128)(2,1)S(1)}, bf16[1,8192]{1,0:T(2,128)(2,1)S(1)}, u32[]{:S(2)}, u32[]{:S(2)}) collective-permute-start(bf16[1,8192]{1,0:T(2,128)(2,1)S(1)} %get-tuple-element.38), channel_id=1, source_target_pairs={{0,2},{1,3},{2,4},{3,5},{4,6},{5,7},{6,8},{7,9},{8,10},{9,11},{10,... | collective-permute-start | bytes 49160 | tf_op jit(solution)/shard_map/ppermute | solution.py:21
  46.5 32.3 %collective-permute-start.6 = (bf16[1,8192]{1,0:T(2,128)(2,1)S(1)}, bf16[1,8192]{1,0:T(2,128)(2,1)S(1)}, u32[]{:S(2)}, u32[]{:S(2)}) collective-permute-start(bf16[1,8192]{1,0:T(2,128)(2,1)S(1)} %get-tuple-element.39), channel_id=1, source_target_pairs={{0,3},{1,4},{2,5},{3,6},{4,7},{5,8},{6,9},{7,10},{8,11},{9,12},{10... | collective-permute-start | bytes 49160 | tf_op jit(solution)/shard_map/ppermute | solution.py:21

commit v5 on v4

--- a/solution.py
+++ b/solution.py
@@ -31,17 +31,17 @@
     return first, second
 
 
-def pack_kernel(offsets, moves_ref, table_ref, pool_ref, *refs):
+def pack_kernel(cuts, moves_ref, table_ref, pool_ref, *refs):
     outs, sems = refs[:-1], refs[-1]
     copies = []
-    for at, offset in enumerate(offsets):
+    for at, (offset, first, some) in enumerate(cuts):
         mover = jnp.int32(0)
         for session in range(1, table_ref.shape[0]):
             mover = jnp.where(moves_ref[session] == offset, jnp.int32(session), mover)
-        for page in range(table_ref.shape[1]):
+        for page in range(some):
             copies.append(
                 pltpu.make_async_copy(
-                    pool_ref.at[table_ref[mover, page]], outs[at].at[page], sems.at[at, page]
+                    pool_ref.at[table_ref[mover, first + page]], outs[at].at[page], sems.at[at, page]
                 )
             )
             copies[-1].start()
@@ -49,19 +49,21 @@
         copy.wait()
 
 
-def pack(offsets, moves, page_table, kv_pool):
-    pages = page_table.shape[1]
-    piece = jax.ShapeDtypeStruct((pages,) + kv_pool.shape[1:], kv_pool.dtype)
+def pack(cuts, moves, page_table, kv_pool):
+    shapes = tuple(
+        jax.ShapeDtypeStruct((some,) + kv_pool.shape[1:], kv_pool.dtype) for _, _, some in cuts
+    )
+    most = max(some for _, _, some in cuts)
     return pl.pallas_call(
-        functools.partial(pack_kernel, offsets),
-        out_shape=(piece,) * len(offsets),
+        functools.partial(pack_kernel, cuts),
+        out_shape=shapes,
         in_specs=[
             pl.BlockSpec(memory_space=pltpu.SMEM),
             pl.BlockSpec(memory_space=pltpu.SMEM),
             pl.BlockSpec(memory_space=pltpu.HBM),
         ],
-        out_specs=(pl.BlockSpec(memory_space=pl.ANY),) * len(offsets),
-        scratch_shapes=[pltpu.SemaphoreType.DMA((len(offsets), pages))],
+        out_specs=(pl.BlockSpec(memory_space=pl.ANY),) * len(cuts),
+        scratch_shapes=[pltpu.SemaphoreType.DMA((len(cuts), most))],
         compiler_params=pltpu.CompilerParams(vmem_limit_bytes=LITTLE),
         cost_estimate=SMALL,
         name="pack",
@@ -82,7 +84,8 @@
         )
         copies[-1].start()
     if guests:
-        held[...] = jnp.concatenate([guest[...] for guest in guest_refs], axis=0)
+        one, two = (guest[...] for guest in guest_refs)
+        held[...] = jnp.concatenate([one[:1], two[:1], one[1:]], axis=0)
         copies.append(pltpu.make_async_copy(held, guest_out_ref, guest_sem))
         copies[-1].start()
     for copy in copies:
@@ -98,7 +101,7 @@
     shapes = [pltpu.HBM((total,) + pieces[0].shape[1:], pieces[0].dtype)]
     scratch = [pltpu.SemaphoreType.DMA((len(pieces),))]
     if guests:
-        guest = (len(guests), guests[0].shape[1])
+        guest = (REACH, guests[0].shape[1])
         shapes.append(pltpu.HBM(guest, guests[0].dtype))
         scratch = [pltpu.VMEM(guest, guests[0].dtype)] + scratch + [pltpu.SemaphoreType.DMA]
     return pl.pallas_call(
@@ -117,8 +120,7 @@
 
 
 def attend_kernel(moves_ref, table_ref, lengths_ref, pool_ref, query_ref, fresh_ref, *refs):
-    out_ref, guest_refs = refs[0], refs[1 : 1 + REACH]
-    held, asked, answered, sems = refs[1 + REACH :]
+    out_ref, near_ref, far_ref, held, asked, answered, sems = refs
     sessions, pages = table_ref.shape
     span = pages * held.shape[2]
     reads = []
@@ -189,21 +191,27 @@
         second = answered[head, pl.ds(sessions, sessions)]
         out_ref[0, :, lanes] = first.astype(jnp.bfloat16)
         out_ref[1, :, lanes] = jnp.where(distance > 0, 0.0, second).astype(jnp.bfloat16)
-        for offset in range(1, REACH + 1):
-            row = jnp.sum(jnp.where(distance == offset, second, 0.0), axis=0, keepdims=True)
-            guest_refs[offset - 1][:, lanes] = row.astype(jnp.bfloat16)
+        leaving = [
+            jnp.sum(jnp.where(distance == offset, second, 0.0), axis=0, keepdims=True)
+            for offset in range(1, REACH + 1)
+        ]
+        near_ref[:, lanes] = leaving[0].astype(jnp.bfloat16)
+        far_ref[:, lanes] = jnp.concatenate(leaving[1:], axis=0).astype(jnp.bfloat16)
 
 
 def attend(kv_pool, page_table, lengths, moves, query, new_kv):
     sessions, pages = page_table.shape
-    guest = jax.ShapeDtypeStruct((1, query.shape[2]), query.dtype)
+    shapes = tuple(
+        jax.ShapeDtypeStruct(shape, query.dtype)
+        for shape in (query.shape, (1, query.shape[2]), (REACH - 1, query.shape[2]))
+    )
     return pl.pallas_call(
         attend_kernel,
-        out_shape=(jax.ShapeDtypeStruct(query.shape, query.dtype),) + (guest,) * REACH,
+        out_shape=shapes,
         in_specs=[pl.BlockSpec(memory_space=pltpu.SMEM)] * 3
         + [pl.BlockSpec(memory_space=pltpu.HBM)]
         + [pl.BlockSpec(memory_space=pltpu.VMEM)] * 2,
-        out_specs=(pl.BlockSpec(memory_space=pltpu.VMEM),) * (1 + REACH),
+        out_specs=(pl.BlockSpec(memory_space=pltpu.VMEM),) * len(shapes),
         scratch_shapes=[
             pltpu.VMEM((sessions, pages) + kv_pool.shape[1:], kv_pool.dtype),
             pltpu.VMEM((HQ, STEPS * sessions, HD), jnp.float32),
@@ -221,33 +229,56 @@
     )
 
 
+def join_kernel(own_ref, through_ref, out_ref):
+    out_ref[...] = jnp.concatenate([own_ref[...], through_ref[1:]], axis=0)
+
+
+def join(own, through):
+    return pl.pallas_call(
+        join_kernel,
+        out_shape=jax.ShapeDtypeStruct(through.shape, through.dtype),
+        in_specs=[pl.BlockSpec(memory_space=pltpu.VMEM)] * 2,
+        out_specs=pl.BlockSpec(memory_space=pltpu.VMEM),
+        compiler_params=pltpu.CompilerParams(vmem_limit_bytes=LITTLE),
+        cost_estimate=SMALL,
+        name="join",
+    )(own, through)
+
+
 def body(kv_pool, page_table, lengths, query, new_kv, moves):
     count = lax.axis_size("inst")
     sessions, pages = page_table.shape
     total = REACH * pages
-    near, far = pack((1, 3), moves, page_table, kv_pool)
+    near, far = pack(((1, 0, pages - 1), (3, 0, pages)), moves, page_table, kv_pool)
     near, far, table, query, new_kv = lax.optimization_barrier(
         (near, far, page_table, query, new_kv)
     )
-    (middle,) = pack((2,), moves, table, kv_pool)
-    attended, *leaving = attend(kv_pool, table, lengths, moves, query, new_kv)
-    attended, middle, *leaving = lax.optimization_barrier((attended, middle, *leaving))
+    rest, middle, late = pack(
+        ((1, pages - 1, 1), (2, 0, pages - 1), (2, pages - 1, 1)), moves, table, kv_pool
+    )
+    near = [near, rest]
+    attended, own, ahead = attend(kv_pool, table, lengths, moves, query, new_kv)
+    attended, middle, late, own, ahead = lax.optimization_barrier(
+        (attended, middle, late, own, ahead)
+    )
     if count % 4 == 0:
         hops = relay_pairs(count)
     else:
         hops = (shift_pairs(count, 1),)
-    near = send(near, hops[0])
+    near = [send(part, hops[0]) for part in near]
     far = send(far, shift_pairs(count, 3))
+    ahead = send(ahead, shift_pairs(count, 2))
     middle = send(middle, shift_pairs(count, 2))
-    guests = [
-        send(leaving[offset - 1], shift_pairs(count, offset))
-        for offset in range(1, REACH + 1)
-    ]
     (moved,) = place((far,), (2 * pages,), total)
-    near, moved = lax.optimization_barrier((near, moved))
+    near, ahead, moved = lax.optimization_barrier((near, ahead, moved))
+    rows = join(own, ahead)
     for hop in hops[1:]:
-        near = send(near, hop)
-    moved, guest_attended = place((middle, near), (pages, 0), total, moved, guests)
+        near = [send(part, hop) for part in near]
+    rows = send(rows, shift_pairs(count, 1))
+    late = send(late, shift_pairs(count, 2))
+    (moved,) = place((middle, *near), (pages, 0, pages - 1), total, moved)
+    ahead, moved, late, rows = lax.optimization_barrier((ahead, moved, late, rows))
+    moved, guest_attended = place((late,), (2 * pages - 1,), total, moved, (rows, ahead))
     return attended, guest_attended, moved
 
 

time: 80.8 us -> 79.9 us (0.989)
  waiting for transfers between devices: 45.5 us -> 44.3 us
    ppermute x7 -> x9, waiting for transfers between devices: 45.5 us -> 44.3 us  [send(): return lax.ppermute(value, 'inst', pairs)]
    pallas_call x2 -> x3, Pallas kernels: 2.85 us -> 3.48 us  [place(): pl.pallas_call(functools.partial(place_kernel, rows, len(guests)), out_sh...]
    ppermute x7 -> x9, starting transfers between devices: 12.8 us -> 12.3 us  [send(): return lax.ppermute(value, 'inst', pairs)]
    pallas_call x3 -> x4, Pallas kernels: 18.7 us -> 18.8 us  [the longest x1 14 us: attend(): pl.pallas_call(attend_kernel, out_shape=shapes, in_specs=[pl.BlockSpec(me...]
  transfers between devices with their start and end apart: 7 -> 9, of which waited for: 3 -> 6; matrix products, arithmetic and copies ran while one was open for 0% -> 0% of each run, Pallas kernels for 21% -> 24%
where the time goes in v5:
time: 79.9 us; the launch traced here: 79.6 us
  waiting for transfers between devices  44.3 us (55%)
  Pallas kernels  22.3 us (28%)
  starting transfers between devices  12.3 us (15%)
    ppermute x9, waiting for transfers between devices, send(): return lax.ppermute(value, 'inst', pairs)  44.3 us
    pallas_call x1, Pallas kernels, attend(): pl.pallas_call(attend_kernel, out_shape=shapes, in_specs=[pl.BlockSpec(me...  14 us
    ppermute x9, starting transfers between devices, send(): return lax.ppermute(value, 'inst', pairs)  12.3 us
    pallas_call x2, Pallas kernels, pack(): pl.pallas_call(functools.partial(pack_kernel, cuts), out_shape=shapes, in...  4.71 us
    pallas_call x3, Pallas kernels, place(): pl.pallas_call(functools.partial(place_kernel, rows, len(guests)), out_sh...  3.48 us
  transfers between devices with their start and end apart: 9, of which 6 were waited for; matrix products, arithmetic and copies ran while one was open for 0% of the time, Pallas kernels for 24%

profile of v5, /device:TPU:0, one launch (start us, length us, event | category | flops | bytes accessed | tf_op | source)
XLA Modules:
  0.0 79.6 jit_solution(15011774280925594401)
XLA Ops:
  0.6 2.4 %pack.2 = (bf16[2,128,2048]{2,1,0:T(8,128)(2,1)S(1)}, bf16[3,128,2048]{2,1,0:T(8,128)(2,1)S(1)}) custom-call(s32[4]{0:T(128)} %moves_ref.5, s32[4,3]{1,0:T(4,128)} %table_ref.3, bf16[12,128,2048]{2,1,0:T(8,128)(2,1)} %pool_ref.5), custom_call_target="tpu_custom_call" | custom-call | tf_op jit(solution)/shard_map/pack/pallas_call | solution.py:57
  3.1 2.4 %collective-permute-start.3 = (bf16[3,128,2048]{2,1,0:T(8,128)(2,1)S(1)}, bf16[3,128,2048]{2,1,0:T(8,128)(2,1)S(1)}, u32[]{:S(2)}, u32[]{:S(2)}) collective-permute-start(bf16[3,128,2048]{2,1,0:T(8,128)(2,1)S(1)} %get-tuple-element.45), channel_id=1, source_target_pairs={{0,3},{1,4},{2,5},{3,6},{4,7},{5,8},{6,9},{7,10},{8,11},{9,12},{10... | collective-permute-start | bytes 4718600 | tf_op jit(solution)/shard_map/ppermute | solution.py:21
  5.5 0.8 collective-permute-start
  6.3 2.3 %pack.3 = (bf16[1,128,2048]{2,1,0:T(8,128)(2,1)S(1)}, bf16[2,128,2048]{2,1,0:T(8,128)(2,1)S(1)}, bf16[1,128,2048]{2,1,0:T(8,128)(2,1)S(1)}) custom-call(s32[4]{0:T(128)} %moves_ref.5, s32[4,3]{1,0:T(4,128)} %table_ref.3, bf16[12,128,2048]{2,1,0:T(8,128)(2,1)} %pool_ref.5), custom_call_target="tpu_custom_call" | custom-call | tf_op jit(solution)/shard_map/pack/pallas_call | solution.py:57
  8.6 0.9 %collective-permute-start.1 = (bf16[1,128,2048]{2,1,0:T(8,128)(2,1)S(1)}, bf16[1,128,2048]{2,1,0:T(8,128)(2,1)S(1)}, u32[]{:S(2)}, u32[]{:S(2)}) collective-permute-start(bf16[1,128,2048]{2,1,0:T(8,128)(2,1)S(1)} %get-tuple-element.43), channel_id=1, source_target_pairs={{0,1},{1,2},{2,3},{3,0},{4,5},{5,6},{6,7},{7,4},{8,9},{9,10},{10,1... | collective-permute-start | bytes 1572872 | tf_op jit(solution)/shard_map/ppermute | solution.py:21
  9.5 14.0 %attend.1 = (bf16[2,4,8192]{2,1,0:T(4,128)(2,1)}, bf16[1,8192]{1,0:T(2,128)(2,1)S(1)}, bf16[2,8192]{1,0:T(2,128)(2,1)S(1)}) custom-call(s32[4]{0:T(128)} %moves_ref.5, s32[4,3]{1,0:T(4,128)} %table_ref.3, s32[4]{0:T(128)} %lengths_ref.1, bf16[12,128,2048]{2,1,0:T(8,128)(2,1)} %pool_ref.5, bf16[2,4,8192]{2,1,0:T(4,128)(2,1)} %query_ref, ...), custom_call_target="tpu_custom_call" | custom-call | tf_op jit(solution)/shard_map/attend/pallas_call | solution.py:208
  23.5 0.7 collective-permute-start.2
  24.2 2.4 %collective-permute-start.4 = (bf16[2,128,2048]{2,1,0:T(8,128)(2,1)S(1)}, bf16[2,128,2048]{2,1,0:T(8,128)(2,1)S(1)}, u32[]{:S(2)}, u32[]{:S(2)}) collective-permute-start(bf16[2,128,2048]{2,1,0:T(8,128)(2,1)S(1)} %get-tuple-element.47), channel_id=1, source_target_pairs={{0,2},{1,3},{2,4},{3,5},{4,6},{5,7},{6,8},{7,9},{8,10},{9,11},{10,... | collective-permute-start | bytes 3145736 | tf_op jit(solution)/shard_map/ppermute | solution.py:21
  26.6 12.7 %collective-permute-done.3.refs_0_ = bf16[3,128,2048]{2,1,0:T(8,128)(2,1)S(1)} collective-permute-done((bf16[3,128,2048]{2,1,0:T(8,128)(2,1)S(1)}, bf16[3,128,2048]{2,1,0:T(8,128)(2,1)S(1)}, u32[]{:S(2)}, u32[]{:S(2)}) %collective-permute-start.3) | collective-permute-done | bytes 1572896 | tf_op jit(solution)/shard_map/ppermute | solution.py:21
  39.3 1.1 %place.3.refs_3_ = bf16[9,128,2048]{2,1,0:T(8,128)(2,1)} custom-call(bf16[3,128,2048]{2,1,0:T(8,128)(2,1)S(1)} %collective-permute-done.3.refs_0_), custom_call_target="tpu_custom_call" | custom-call | tf_op jit(solution)/shard_map/place/pallas_call | solution.py:107
  40.5 4.5 %collective-permute-done.2.through_ref.refs_2_ = bf16[2,8192]{1,0:T(2,128)(2,1)S(1)} collective-permute-done((bf16[2,8192]{1,0:T(2,128)(2,1)S(1)}, bf16[2,8192]{1,0:T(2,128)(2,1)S(1)}, u32[]{:S(2)}, u32[]{:S(2)}) %collective-permute-start.2) | collective-permute-done | bytes 32800 | tf_op jit(solution)/shard_map/ppermute | solution.py:21
  45.0 0.0 collective-permute-done.1
  45.0 0.0 collective-permute-done
  45.0 1.9 %collective-permute-start.5 = (bf16[2,128,2048]{2,1,0:T(8,128)(2,1)S(1)}, bf16[2,128,2048]{2,1,0:T(8,128)(2,1)S(1)}, u32[]{:S(2)}, u32[]{:S(2)}) collective-permute-start(bf16[2,128,2048]{2,1,0:T(8,128)(2,1)S(1)} %collective-permute-done), channel_id=1, source_target_pairs={{0,4},{1,1},{2,2},{3,3},{4,8},{5,5},{6,6},{7,7},{8,12},{9,9},{10,1... | collective-permute-start | bytes 3145736 | tf_op jit(solution)/shard_map/ppermute | solution.py:21
  46.9 3.0 %collective-permute-start.6 = (bf16[1,128,2048]{2,1,0:T(8,128)(2,1)S(1)}, bf16[1,128,2048]{2,1,0:T(8,128)(2,1)S(1)}, u32[]{:S(2)}, u32[]{:S(2)}) collective-permute-start(bf16[1,128,2048]{2,1,0:T(8,128)(2,1)S(1)} %collective-permute-done.1), channel_id=1, source_target_pairs={{0,4},{1,1},{2,2},{3,3},{4,8},{5,5},{6,6},{7,7},{8,12},{9,9},{10,1... | collective-permute-start | bytes 1572872 | tf_op jit(solution)/shard_map/ppermute | solution.py:21
  49.9 0.1 collective-permute-start.7
  50.0 0.1 join.1
  50.0 0.1 collective-permute-start.8
  50.1 17.3 %collective-permute-done.4.refs_0_ = bf16[2,128,2048]{2,1,0:T(8,128)(2,1)S(1)} collective-permute-done((bf16[2,128,2048]{2,1,0:T(8,128)(2,1)S(1)}, bf16[2,128,2048]{2,1,0:T(8,128)(2,1)S(1)}, u32[]{:S(2)}, u32[]{:S(2)}) %collective-permute-start.4) | collective-permute-done | bytes 1048608 | tf_op jit(solution)/shard_map/ppermute | solution.py:21
  67.4 1.6 %collective-permute-done.6.refs_2_ = bf16[1,128,2048]{2,1,0:T(8,128)(2,1)S(1)} collective-permute-done((bf16[1,128,2048]{2,1,0:T(8,128)(2,1)S(1)}, bf16[1,128,2048]{2,1,0:T(8,128)(2,1)S(1)}, u32[]{:S(2)}, u32[]{:S(2)}) %collective-permute-start.6) | collective-permute-done | bytes 524320 | tf_op jit(solution)/shard_map/ppermute | solution.py:21
  69.1 0.0 collective-permute-done.5.refs_1_
  69.1 1.5 %place.4.refs_3_ = bf16[9,128,2048]{2,1,0:T(8,128)(2,1)} custom-call(bf16[2,128,2048]{2,1,0:T(8,128)(2,1)S(1)} %collective-permute-done.4.refs_0_, bf16[2,128,2048]{2,1,0:T(8,128)(2,1)S(1)} %collective-permute-done.5.refs_1_, bf16[1,128,2048]{2,1,0:T(8,128)(2,1)S(1)} %collective-permute-done.6.refs_2_, ...), custom_call_target="tpu_custom_call", output_to_operand_aliasing={{}: (3, {})} | custom-call | tf_op jit(solution)/shard_map/place/pallas_call | solution.py:107
  70.6 8.1 %collective-permute-done.7.refs_0_ = bf16[1,128,2048]{2,1,0:T(8,128)(2,1)S(1)} collective-permute-done((bf16[1,128,2048]{2,1,0:T(8,128)(2,1)S(1)}, bf16[1,128,2048]{2,1,0:T(8,128)(2,1)S(1)}, u32[]{:S(2)}, u32[]{:S(2)}) %collective-permute-start.7) | collective-permute-done | bytes 524320 | tf_op jit(solution)/shard_map/ppermute | solution.py:21
  78.7 0.1 collective-permute-done.8.refs_1_
  78.8 0.8 %place.5 = (bf16[9,128,2048]{2,1,0:T(8,128)(2,1)}, bf16[3,8192]{1,0:T(4,128)(2,1)}) custom-call(bf16[1,128,2048]{2,1,0:T(8,128)(2,1)S(1)} %collective-permute-done.7.refs_0_, bf16[2,8192]{1,0:T(2,128)(2,1)S(1)} %collective-permute-done.8.refs_1_, bf16[2,8192]{1,0:T(2,128)(2,1)S(1)} %collective-permute-done.2.through_ref.refs_2_, ...), custom_call_target="tpu_custom_call", output_to_operand_aliasing={{0}: (3, {})} | custom-call | tf_op jit(solution)/shard_map/place/pallas_call | solution.py:107
Async XLA Ops:
  3.1 36.2 %collective-permute-start.3 = (bf16[3,128,2048]{2,1,0:T(8,128)(2,1)S(1)}, bf16[3,128,2048]{2,1,0:T(8,128)(2,1)S(1)}, u32[]{:S(2)}, u32[]{:S(2)}) collective-permute-start(bf16[3,128,2048]{2,1,0:T(8,128)(2,1)S(1)} %get-tuple-element.45), channel_id=1, source_target_pairs={{0,3},{1,4},{2,5},{3,6},{4,7},{5,8},{6,9},{7,10},{8,11},{9,12},{10... | collective-permute-start | bytes 4718600 | tf_op jit(solution)/shard_map/ppermute | solution.py:21
  5.5 39.5 %collective-permute-start = (bf16[2,128,2048]{2,1,0:T(8,128)(2,1)S(1)}, bf16[2,128,2048]{2,1,0:T(8,128)(2,1)S(1)}, u32[]{:S(2)}, u32[]{:S(2)}) collective-permute-start(bf16[2,128,2048]{2,1,0:T(8,128)(2,1)S(1)} %get-tuple-element.42), channel_id=1, source_target_pairs={{0,1},{1,2},{2,3},{3,0},{4,5},{5,6},{6,7},{7,4},{8,9},{9,10},{10,1... | collective-permute-start | bytes 3145736 | tf_op jit(solution)/shard_map/ppermute | solution.py:21
  8.6 36.4 %collective-permute-start.1 = (bf16[1,128,2048]{2,1,0:T(8,128)(2,1)S(1)}, bf16[1,128,2048]{2,1,0:T(8,128)(2,1)S(1)}, u32[]{:S(2)}, u32[]{:S(2)}) collective-permute-start(bf16[1,128,2048]{2,1,0:T(8,128)(2,1)S(1)} %get-tuple-element.43), channel_id=1, source_target_pairs={{0,1},{1,2},{2,3},{3,0},{4,5},{5,6},{6,7},{7,4},{8,9},{9,10},{10,1... | collective-permute-start | bytes 1572872 | tf_op jit(solution)/shard_map/ppermute | solution.py:21
  23.5 21.4 %collective-permute-start.2 = (bf16[2,8192]{1,0:T(2,128)(2,1)S(1)}, bf16[2,8192]{1,0:T(2,128)(2,1)S(1)}, u32[]{:S(2)}, u32[]{:S(2)}) collective-permute-start(bf16[2,8192]{1,0:T(2,128)(2,1)S(1)} %get-tuple-element.44), channel_id=1, source_target_pairs={{0,2},{1,3},{2,4},{3,5},{4,6},{5,7},{6,8},{7,9},{8,10},{9,11},{10,... | collective-permute-start | bytes 98312 | tf_op jit(solution)/shard_map/ppermute | solution.py:21
  24.2 43.2 %collective-permute-start.4 = (bf16[2,128,2048]{2,1,0:T(8,128)(2,1)S(1)}, bf16[2,128,2048]{2,1,0:T(8,128)(2,1)S(1)}, u32[]{:S(2)}, u32[]{:S(2)}) collective-permute-start(bf16[2,128,2048]{2,1,0:T(8,128)(2,1)S(1)} %get-tuple-element.47), channel_id=1, source_target_pairs={{0,2},{1,3},{2,4},{3,5},{4,6},{5,7},{6,8},{7,9},{8,10},{9,11},{10,... | collective-permute-start | bytes 3145736 | tf_op jit(solution)/shard_map/ppermute | solution.py:21
  45.0 24.1 %collective-permute-start.5 = (bf16[2,128,2048]{2,1,0:T(8,128)(2,1)S(1)}, bf16[2,128,2048]{2,1,0:T(8,128)(2,1)S(1)}, u32[]{:S(2)}, u32[]{:S(2)}) collective-permute-start(bf16[2,128,2048]{2,1,0:T(8,128)(2,1)S(1)} %collective-permute-done), channel_id=1, source_target_pairs={{0,4},{1,1},{2,2},{3,3},{4,8},{5,5},{6,6},{7,7},{8,12},{9,9},{10,1... | collective-permute-start | bytes 3145736 | tf_op jit(solution)/shard_map/ppermute | solution.py:21
  46.9 22.2 %collective-permute-start.6 = (bf16[1,128,2048]{2,1,0:T(8,128)(2,1)S(1)}, bf16[1,128,2048]{2,1,0:T(8,128)(2,1)S(1)}, u32[]{:S(2)}, u32[]{:S(2)}) collective-permute-start(bf16[1,128,2048]{2,1,0:T(8,128)(2,1)S(1)} %collective-permute-done.1), channel_id=1, source_target_pairs={{0,4},{1,1},{2,2},{3,3},{4,8},{5,5},{6,6},{7,7},{8,12},{9,9},{10,1... | collective-permute-start | bytes 1572872 | tf_op jit(solution)/shard_map/ppermute | solution.py:21
  49.9 28.8 %collective-permute-start.7 = (bf16[1,128,2048]{2,1,0:T(8,128)(2,1)S(1)}, bf16[1,128,2048]{2,1,0:T(8,128)(2,1)S(1)}, u32[]{:S(2)}, u32[]{:S(2)}) collective-permute-start(bf16[1,128,2048]{2,1,0:T(8,128)(2,1)S(1)} %get-tuple-element.51), channel_id=1, source_target_pairs={{0,2},{1,3},{2,4},{3,5},{4,6},{5,7},{6,8},{7,9},{8,10},{9,11},{10,... | collective-permute-start | bytes 1572872 | tf_op jit(solution)/shard_map/ppermute | solution.py:21
  50.0 28.7 %collective-permute-start.8 = (bf16[2,8192]{1,0:T(2,128)(2,1)S(1)}, bf16[2,8192]{1,0:T(2,128)(2,1)S(1)}, u32[]{:S(2)}, u32[]{:S(2)}) collective-permute-start(bf16[2,8192]{1,0:T(2,128)(2,1)S(1)} %join.1), channel_id=1, source_target_pairs={{0,1},{1,2},{2,3},{3,4},{4,5},{5,6},{6,7},{7,8},{8,9},{9,10},{10,1... | collective-permute-start | bytes 98312 | tf_op jit(solution)/shard_map/ppermute | solution.py:21

commit v6 on v4

--- a/solution.py
+++ b/solution.py
@@ -15,6 +15,8 @@
 STEPS = 2
 SMALL = pl.CostEstimate(flops=0, bytes_accessed=0, transcendentals=0)
 LITTLE = 1 << 20
+LINES = 8
+PIECES = 2
 
 
 def send(value, pairs):
@@ -31,41 +33,46 @@
     return first, second
 
 
-def pack_kernel(offsets, moves_ref, table_ref, pool_ref, *refs):
+def pack_kernel(cuts, moves_ref, table_ref, pool_ref, *refs):
     outs, sems = refs[:-1], refs[-1]
     copies = []
-    for at, offset in enumerate(offsets):
+    for at, (offset, first, some) in enumerate(cuts):
         mover = jnp.int32(0)
         for session in range(1, table_ref.shape[0]):
             mover = jnp.where(moves_ref[session] == offset, jnp.int32(session), mover)
-        for page in range(table_ref.shape[1]):
+        piece = first
+        while piece < first + some:
+            span = min(PIECES - piece % PIECES, first + some - piece)
+            slot = table_ref[mover, piece // PIECES] * PIECES + piece % PIECES
             copies.append(
                 pltpu.make_async_copy(
-                    pool_ref.at[table_ref[mover, page]], outs[at].at[page], sems.at[at, page]
+                    pool_ref.at[pl.ds(slot, span)],
+                    outs[at].at[pl.ds(piece - first, span)],
+                    sems.at[at, piece // PIECES - first // PIECES],
                 )
             )
             copies[-1].start()
+            piece += span
     for copy in copies:
         copy.wait()
 
 
-def pack(offsets, moves, page_table, kv_pool):
-    pages = page_table.shape[1]
-    piece = jax.ShapeDtypeStruct((pages,) + kv_pool.shape[1:], kv_pool.dtype)
+def pack(cuts, moves, page_table, pool):
+    shapes = tuple(jax.ShapeDtypeStruct((some,) + pool.shape[1:], pool.dtype) for _, _, some in cuts)
     return pl.pallas_call(
-        functools.partial(pack_kernel, offsets),
-        out_shape=(piece,) * len(offsets),
+        functools.partial(pack_kernel, cuts),
+        out_shape=shapes,
         in_specs=[
             pl.BlockSpec(memory_space=pltpu.SMEM),
             pl.BlockSpec(memory_space=pltpu.SMEM),
             pl.BlockSpec(memory_space=pltpu.HBM),
         ],
-        out_specs=(pl.BlockSpec(memory_space=pl.ANY),) * len(offsets),
-        scratch_shapes=[pltpu.SemaphoreType.DMA((len(offsets), pages))],
+        out_specs=(pl.BlockSpec(memory_space=pl.ANY),) * len(cuts),
+        scratch_shapes=[pltpu.SemaphoreType.DMA((len(cuts), page_table.shape[1]))],
         compiler_params=pltpu.CompilerParams(vmem_limit_bytes=LITTLE),
         cost_estimate=SMALL,
         name="pack",
-    )(*(pltpu.with_memory_space_constraint(x, pltpu.HBM) for x in (moves, page_table, kv_pool)))
+    )(*(pltpu.with_memory_space_constraint(x, pltpu.HBM) for x in (moves, page_table, pool)))
 
 
 def place_kernel(rows, guests, *refs):
@@ -82,7 +89,11 @@
         )
         copies[-1].start()
     if guests:
-        held[...] = jnp.concatenate([guest[...] for guest in guest_refs], axis=0)
+        wide = [guest[...].astype(jnp.float32) for guest in guest_refs]
+        for line in range(wide[0].shape[0]):
+            lanes = pl.ds(line * wide[0].shape[1], wide[0].shape[1])
+            rows = [guest[line : line + 1] for guest in wide]
+            held[:, lanes] = jnp.concatenate(rows, axis=0).astype(held.dtype)
         copies.append(pltpu.make_async_copy(held, guest_out_ref, guest_sem))
         copies[-1].start()
     for copy in copies:
@@ -98,7 +109,7 @@
     shapes = [pltpu.HBM((total,) + pieces[0].shape[1:], pieces[0].dtype)]
     scratch = [pltpu.SemaphoreType.DMA((len(pieces),))]
     if guests:
-        guest = (len(guests), guests[0].shape[1])
+        guest = (REACH, guests[0].size)
         shapes.append(pltpu.HBM(guest, guests[0].dtype))
         scratch = [pltpu.VMEM(guest, guests[0].dtype)] + scratch + [pltpu.SemaphoreType.DMA]
     return pl.pallas_call(
@@ -118,7 +129,7 @@
 
 def attend_kernel(moves_ref, table_ref, lengths_ref, pool_ref, query_ref, fresh_ref, *refs):
     out_ref, guest_refs = refs[0], refs[1 : 1 + REACH]
-    held, asked, answered, sems = refs[1 + REACH :]
+    held, asked, answered, leaving, sems = refs[1 + REACH :]
     sessions, pages = table_ref.shape
     span = pages * held.shape[2]
     reads = []
@@ -191,23 +202,29 @@
         out_ref[1, :, lanes] = jnp.where(distance > 0, 0.0, second).astype(jnp.bfloat16)
         for offset in range(1, REACH + 1):
             row = jnp.sum(jnp.where(distance == offset, second, 0.0), axis=0, keepdims=True)
-            guest_refs[offset - 1][:, lanes] = row.astype(jnp.bfloat16)
+            leaving[offset - 1, pl.ds(head // LINES, 1), pl.ds(head % LINES * HD, HD)] = row
+    for at, guest_ref in enumerate(guest_refs):
+        guest_ref[...] = leaving[at].astype(jnp.bfloat16)
 
 
 def attend(kv_pool, page_table, lengths, moves, query, new_kv):
     sessions, pages = page_table.shape
-    guest = jax.ShapeDtypeStruct((1, query.shape[2]), query.dtype)
+    shapes = tuple(
+        jax.ShapeDtypeStruct(shape, query.dtype)
+        for shape in (query.shape,) + ((HQ // LINES, LINES * HD),) * REACH
+    )
     return pl.pallas_call(
         attend_kernel,
-        out_shape=(jax.ShapeDtypeStruct(query.shape, query.dtype),) + (guest,) * REACH,
+        out_shape=shapes,
         in_specs=[pl.BlockSpec(memory_space=pltpu.SMEM)] * 3
         + [pl.BlockSpec(memory_space=pltpu.HBM)]
         + [pl.BlockSpec(memory_space=pltpu.VMEM)] * 2,
-        out_specs=(pl.BlockSpec(memory_space=pltpu.VMEM),) * (1 + REACH),
+        out_specs=(pl.BlockSpec(memory_space=pltpu.VMEM),) * len(shapes),
         scratch_shapes=[
             pltpu.VMEM((sessions, pages) + kv_pool.shape[1:], kv_pool.dtype),
             pltpu.VMEM((HQ, STEPS * sessions, HD), jnp.float32),
             pltpu.VMEM((HQ, STEPS * sessions, HD), jnp.float32),
+            pltpu.VMEM((REACH, HQ // LINES, LINES * HD), jnp.float32),
             pltpu.SemaphoreType.DMA((sessions, pages)),
         ],
         compiler_params=pltpu.CompilerParams(vmem_limit_bytes=16 << 20),
@@ -221,34 +238,67 @@
     )
 
 
+def split_kernel(whole_ref, *refs):
+    outs, sems = refs[:-1], refs[-1]
+    copies, row = [], 0
+    for at, out in enumerate(outs):
+        copies.append(
+            pltpu.make_async_copy(whole_ref.at[pl.ds(row, out.shape[0])], out, sems.at[at])
+        )
+        copies[-1].start()
+        row += out.shape[0]
+    for copy in copies:
+        copy.wait()
+
+
+def split(whole, sizes):
+    return pl.pallas_call(
+        split_kernel,
+        out_shape=tuple(
+            jax.ShapeDtypeStruct((size,) + whole.shape[1:], whole.dtype) for size in sizes
+        ),
+        in_specs=[pl.BlockSpec(memory_space=pl.ANY)],
+        out_specs=(pl.BlockSpec(memory_space=pl.ANY),) * len(sizes),
+        scratch_shapes=[pltpu.SemaphoreType.DMA((len(sizes),))],
+        compiler_params=pltpu.CompilerParams(vmem_limit_bytes=LITTLE),
+        cost_estimate=SMALL,
+        name="split",
+    )(whole)
+
+
 def body(kv_pool, page_table, lengths, query, new_kv, moves):
     count = lax.axis_size("inst")
     sessions, pages = page_table.shape
-    total = REACH * pages
-    near, far = pack((1, 3), moves, page_table, kv_pool)
+    each = pages * PIECES
+    total = REACH * each
+    pool = kv_pool.reshape(-1, kv_pool.shape[1] // PIECES, kv_pool.shape[2])
+    near, far = pack(((1, 0, each), (3, 0, each)), moves, page_table, pool)
     near, far, table, query, new_kv = lax.optimization_barrier(
         (near, far, page_table, query, new_kv)
     )
-    (middle,) = pack((2,), moves, table, kv_pool)
-    attended, *leaving = attend(kv_pool, table, lengths, moves, query, new_kv)
-    attended, middle, *leaving = lax.optimization_barrier((attended, middle, *leaving))
+    middle, late = pack(((2, 0, each - 1), (2, each - 1, 1)), moves, table, pool)
+    attended, *guests = attend(kv_pool, table, lengths, moves, query, new_kv)
+    attended, middle, late, *guests = lax.optimization_barrier((attended, middle, late, *guests))
     if count % 4 == 0:
         hops = relay_pairs(count)
     else:
         hops = (shift_pairs(count, 1),)
     near = send(near, hops[0])
     far = send(far, shift_pairs(count, 3))
+    two = send(guests[1], shift_pairs(count, 2))
+    three = send(guests[2], shift_pairs(count, 3))
     middle = send(middle, shift_pairs(count, 2))
-    guests = [
-        send(leaving[offset - 1], shift_pairs(count, offset))
-        for offset in range(1, REACH + 1)
-    ]
-    (moved,) = place((far,), (2 * pages,), total)
-    near, moved = lax.optimization_barrier((near, moved))
+    (moved,) = place((far,), (2 * each,), total)
+    near, two, three, one, moved = lax.optimization_barrier((near, two, three, guests[0], moved))
+    near = split(near, (each - 1, 1))
     for hop in hops[1:]:
-        near = send(near, hop)
-    moved, guest_attended = place((middle, near), (pages, 0), total, moved, guests)
-    return attended, guest_attended, moved
+        near = [send(part, hop) for part in near]
+    one = send(one, shift_pairs(count, 1))
+    late = send(late, shift_pairs(count, 2))
+    (moved,) = place((middle, *near), (each, 0, each - 1), total, moved)
+    two, three, moved, late, one = lax.optimization_barrier((two, three, moved, late, one))
+    moved, guest_attended = place((late,), (2 * each - 1,), total, moved, (one, two, three))
+    return attended, guest_attended, moved.reshape(-1, *kv_pool.shape[1:])
 
 
 def solution(mesh):

time: 80.8 us -> 79.8 us (0.988)
  waiting for transfers between devices: 45.5 us -> 44.3 us
    ppermute x7 -> x9, waiting for transfers between devices: 45.5 us -> 44.3 us  [send(): return lax.ppermute(value, 'inst', pairs)]
    ppermute x7 -> x9, starting transfers between devices: 12.8 us -> 12.2 us  [send(): return lax.ppermute(value, 'inst', pairs)]
    pallas_call x2 -> x3, Pallas kernels: 2.85 us -> 3.48 us  [place(): pl.pallas_call(functools.partial(place_kernel, rows, len(guests)), out_sh...]
    pallas_call x3 -> x4, Pallas kernels: 18.7 us -> 18.8 us  [the longest x1 14 us: attend(): pl.pallas_call(attend_kernel, out_shape=shapes, in_specs=[pl.BlockSpec(me...]
  transfers between devices with their start and end apart: 7 -> 9, of which waited for: 3 -> 4; matrix products, arithmetic and copies ran while one was open for 0% -> 0% of each run, Pallas kernels for 21% -> 24%
where the time goes in v6:
time: 79.8 us; the launch traced here: 79.5 us
  waiting for transfers between devices  44.3 us (56%)
  Pallas kernels  22.3 us (28%)
  starting transfers between devices  12.2 us (15%)
    ppermute x9, waiting for transfers between devices, send(): return lax.ppermute(value, 'inst', pairs)  44.3 us
    pallas_call x1, Pallas kernels, attend(): pl.pallas_call(attend_kernel, out_shape=shapes, in_specs=[pl.BlockSpec(me...  14 us
    ppermute x9, starting transfers between devices, send(): return lax.ppermute(value, 'inst', pairs)  12.2 us
    pallas_call x2, Pallas kernels, pack(): pl.pallas_call(functools.partial(pack_kernel, cuts), out_shape=shapes, in...  4.7 us
    pallas_call x3, Pallas kernels, place(): pl.pallas_call(functools.partial(place_kernel, rows, len(guests)), out_sh...  3.48 us
  transfers between devices with their start and end apart: 9, of which 4 were waited for; matrix products, arithmetic and copies ran while one was open for 0% of the time, Pallas kernels for 24%

profile of v6, /device:TPU:0, one launch (start us, length us, event | category | flops | bytes accessed | tf_op | source)
XLA Modules:
  0.0 79.5 jit_solution(17155979756741004780)
XLA Ops:
  0.6 2.6 %pack.2 = (bf16[6,64,2048]{2,1,0:T(8,128)(2,1)S(1)}, bf16[6,64,2048]{2,1,0:T(8,128)(2,1)S(1)}) custom-call(s32[4]{0:T(128)} %moves_ref.5, s32[4,3]{1,0:T(4,128)} %table_ref.3, bf16[24,64,2048]{2,1,0:T(8,128)(2,1)} %bitcast.2), custom_call_target="tpu_custom_call" | custom-call | tf_op jit(solution)/shard_map/pack/pallas_call | solution.py:62
  3.2 2.4 %collective-permute-start.3 = (bf16[6,64,2048]{2,1,0:T(8,128)(2,1)S(1)}, bf16[6,64,2048]{2,1,0:T(8,128)(2,1)S(1)}, u32[]{:S(2)}, u32[]{:S(2)}) collective-permute-start(bf16[6,64,2048]{2,1,0:T(8,128)(2,1)S(1)} %get-tuple-element.52), channel_id=1, source_target_pairs={{0,3},{1,4},{2,5},{3,6},{4,7},{5,8},{6,9},{7,10},{8,11},{9,12},{10... | collective-permute-start | bytes 4718600 | tf_op jit(solution)/shard_map/ppermute | solution.py:23
  5.7 0.8 collective-permute-start
  6.4 2.1 %pack.3 = (bf16[5,64,2048]{2,1,0:T(8,128)(2,1)S(1)}, bf16[1,64,2048]{2,1,0:T(8,128)(2,1)S(1)}) custom-call(s32[4]{0:T(128)} %moves_ref.5, s32[4,3]{1,0:T(4,128)} %table_ref.3, bf16[24,64,2048]{2,1,0:T(8,128)(2,1)} %bitcast.3), custom_call_target="tpu_custom_call" | custom-call | tf_op jit(solution)/shard_map/pack/pallas_call | solution.py:62
  8.5 14.0 %attend.1 = (bf16[2,4,8192]{2,1,0:T(4,128)(2,1)}, bf16[8,1024]{1,0:T(8,128)(2,1)S(1)}, bf16[8,1024]{1,0:T(8,128)(2,1)S(1)}, bf16[8,1024]{1,0:T(8,128)(2,1)S(1)}) custom-call(s32[4]{0:T(128)} %moves_ref.5, s32[4,3]{1,0:T(4,128)} %table_ref.3, s32[4]{0:T(128)} %lengths_ref.1, bf16[12,128,2048]{2,1,0:T(8,128)(2,1)} %pool_ref.1, bf16[2,4,8192]{2,1,0:T(4,128)(2,1)} %query_ref, ...), custom_call_target="tpu_custom_call" | custom-call | tf_op jit(solution)/shard_map/attend/pallas_call | solution.py:216
  22.5 1.5 %collective-permute-start.1 = (bf16[8,1024]{1,0:T(8,128)(2,1)S(1)}, bf16[8,1024]{1,0:T(8,128)(2,1)S(1)}, u32[]{:S(2)}, u32[]{:S(2)}) collective-permute-start(bf16[8,1024]{1,0:T(8,128)(2,1)S(1)} %get-tuple-element.49), channel_id=1, source_target_pairs={{0,2},{1,3},{2,4},{3,5},{4,6},{5,7},{6,8},{7,9},{8,10},{9,11},{10,... | collective-permute-start | bytes 49160 | tf_op jit(solution)/shard_map/ppermute | solution.py:23
  24.1 1.8 %collective-permute-start.2 = (bf16[8,1024]{1,0:T(8,128)(2,1)S(1)}, bf16[8,1024]{1,0:T(8,128)(2,1)S(1)}, u32[]{:S(2)}, u32[]{:S(2)}) collective-permute-start(bf16[8,1024]{1,0:T(8,128)(2,1)S(1)} %get-tuple-element.50), channel_id=1, source_target_pairs={{0,3},{1,4},{2,5},{3,6},{4,7},{5,8},{6,9},{7,10},{8,11},{9,12},{10... | collective-permute-start | bytes 49160 | tf_op jit(solution)/shard_map/ppermute | solution.py:23
  25.9 0.6 collective-permute-start.4
  26.4 13.0 %collective-permute-done.3.refs_0_ = bf16[6,64,2048]{2,1,0:T(8,128)(2,1)S(1)} collective-permute-done((bf16[6,64,2048]{2,1,0:T(8,128)(2,1)S(1)}, bf16[6,64,2048]{2,1,0:T(8,128)(2,1)S(1)}, u32[]{:S(2)}, u32[]{:S(2)}) %collective-permute-start.3) | collective-permute-done | bytes 1572896 | tf_op jit(solution)/shard_map/ppermute | solution.py:23
  39.5 1.1 %place.3.refs_3_ = bf16[18,64,2048]{2,1,0:T(8,128)(2,1)} custom-call(bf16[6,64,2048]{2,1,0:T(8,128)(2,1)S(1)} %collective-permute-done.3.refs_0_), custom_call_target="tpu_custom_call" | custom-call | tf_op jit(solution)/shard_map/place/pallas_call | solution.py:115
  40.6 4.1 %collective-permute-done.1.refs_2_ = bf16[8,1024]{1,0:T(8,128)(2,1)S(1)} collective-permute-done((bf16[8,1024]{1,0:T(8,128)(2,1)S(1)}, bf16[8,1024]{1,0:T(8,128)(2,1)S(1)}, u32[]{:S(2)}, u32[]{:S(2)}) %collective-permute-start.1) | collective-permute-done | bytes 16416 | tf_op jit(solution)/shard_map/ppermute | solution.py:23
  44.8 0.0 collective-permute-done.2.refs_3_
  44.8 0.0 collective-permute-done.whole_ref
  44.8 0.1 split.1
  44.9 1.9 %collective-permute-start.5 = (bf16[5,64,2048]{2,1,0:T(8,128)(2,1)S(1)}, bf16[5,64,2048]{2,1,0:T(8,128)(2,1)S(1)}, u32[]{:S(2)}, u32[]{:S(2)}) collective-permute-start(bf16[5,64,2048]{2,1,0:T(8,128)(2,1)S(1)} %get-tuple-element.57), channel_id=1, source_target_pairs={{0,4},{1,1},{2,2},{3,3},{4,8},{5,5},{6,6},{7,7},{8,12},{9,9},{10,1... | collective-permute-start | bytes 3932168 | tf_op jit(solution)/shard_map/ppermute | solution.py:23
  46.8 3.0 %collective-permute-start.6 = (bf16[1,64,2048]{2,1,0:T(8,128)(2,1)S(1)}, bf16[1,64,2048]{2,1,0:T(8,128)(2,1)S(1)}, u32[]{:S(2)}, u32[]{:S(2)}) collective-permute-start(bf16[1,64,2048]{2,1,0:T(8,128)(2,1)S(1)} %get-tuple-element.58), channel_id=1, source_target_pairs={{0,4},{1,1},{2,2},{3,3},{4,8},{5,5},{6,6},{7,7},{8,12},{9,9},{10,1... | collective-permute-start | bytes 786440 | tf_op jit(solution)/shard_map/ppermute | solution.py:23
  49.9 0.1 collective-permute-start.7
  49.9 0.1 collective-permute-start.8
  50.0 23.2 %collective-permute-done.4.refs_0_ = bf16[5,64,2048]{2,1,0:T(8,128)(2,1)S(1)} collective-permute-done((bf16[5,64,2048]{2,1,0:T(8,128)(2,1)S(1)}, bf16[5,64,2048]{2,1,0:T(8,128)(2,1)S(1)}, u32[]{:S(2)}, u32[]{:S(2)}) %collective-permute-start.4) | collective-permute-done | bytes 1310752 | tf_op jit(solution)/shard_map/ppermute | solution.py:23
  73.2 0.0 collective-permute-done.6.refs_2_
  73.2 0.0 collective-permute-done.5.refs_1_
  73.2 1.6 %place.4.refs_4_ = bf16[18,64,2048]{2,1,0:T(8,128)(2,1)} custom-call(bf16[5,64,2048]{2,1,0:T(8,128)(2,1)S(1)} %collective-permute-done.4.refs_0_, bf16[5,64,2048]{2,1,0:T(8,128)(2,1)S(1)} %collective-permute-done.5.refs_1_, bf16[1,64,2048]{2,1,0:T(8,128)(2,1)S(1)} %collective-permute-done.6.refs_2_, ...), custom_call_target="tpu_custom_call", output_to_operand_aliasing={{}: (3, {})} | custom-call | tf_op jit(solution)/shard_map/place/pallas_call | solution.py:115
  74.8 3.9 %collective-permute-done.7.refs_0_ = bf16[1,64,2048]{2,1,0:T(8,128)(2,1)S(1)} collective-permute-done((bf16[1,64,2048]{2,1,0:T(8,128)(2,1)S(1)}, bf16[1,64,2048]{2,1,0:T(8,128)(2,1)S(1)}, u32[]{:S(2)}, u32[]{:S(2)}) %collective-permute-start.7) | collective-permute-done | bytes 262176 | tf_op jit(solution)/shard_map/ppermute | solution.py:23
  78.7 0.0 collective-permute-done.8.refs_1_
  78.7 0.7 place.5
Async XLA Ops:
  3.2 36.2 %collective-permute-start.3 = (bf16[6,64,2048]{2,1,0:T(8,128)(2,1)S(1)}, bf16[6,64,2048]{2,1,0:T(8,128)(2,1)S(1)}, u32[]{:S(2)}, u32[]{:S(2)}) collective-permute-start(bf16[6,64,2048]{2,1,0:T(8,128)(2,1)S(1)} %get-tuple-element.52), channel_id=1, source_target_pairs={{0,3},{1,4},{2,5},{3,6},{4,7},{5,8},{6,9},{7,10},{8,11},{9,12},{10... | collective-permute-start | bytes 4718600 | tf_op jit(solution)/shard_map/ppermute | solution.py:23
  5.7 39.1 %collective-permute-start = (bf16[6,64,2048]{2,1,0:T(8,128)(2,1)S(1)}, bf16[6,64,2048]{2,1,0:T(8,128)(2,1)S(1)}, u32[]{:S(2)}, u32[]{:S(2)}) collective-permute-start(bf16[6,64,2048]{2,1,0:T(8,128)(2,1)S(1)} %get-tuple-element.48), channel_id=1, source_target_pairs={{0,1},{1,2},{2,3},{3,0},{4,5},{5,6},{6,7},{7,4},{8,9},{9,10},{10,1... | collective-permute-start | bytes 4718600 | tf_op jit(solution)/shard_map/ppermute | solution.py:23
  22.5 22.2 %collective-permute-start.1 = (bf16[8,1024]{1,0:T(8,128)(2,1)S(1)}, bf16[8,1024]{1,0:T(8,128)(2,1)S(1)}, u32[]{:S(2)}, u32[]{:S(2)}) collective-permute-start(bf16[8,1024]{1,0:T(8,128)(2,1)S(1)} %get-tuple-element.49), channel_id=1, source_target_pairs={{0,2},{1,3},{2,4},{3,5},{4,6},{5,7},{6,8},{7,9},{8,10},{9,11},{10,... | collective-permute-start | bytes 49160 | tf_op jit(solution)/shard_map/ppermute | solution.py:23
  24.1 20.7 %collective-permute-start.2 = (bf16[8,1024]{1,0:T(8,128)(2,1)S(1)}, bf16[8,1024]{1,0:T(8,128)(2,1)S(1)}, u32[]{:S(2)}, u32[]{:S(2)}) collective-permute-start(bf16[8,1024]{1,0:T(8,128)(2,1)S(1)} %get-tuple-element.50), channel_id=1, source_target_pairs={{0,3},{1,4},{2,5},{3,6},{4,7},{5,8},{6,9},{7,10},{8,11},{9,12},{10... | collective-permute-start | bytes 49160 | tf_op jit(solution)/shard_map/ppermute | solution.py:23
  25.9 47.3 %collective-permute-start.4 = (bf16[5,64,2048]{2,1,0:T(8,128)(2,1)S(1)}, bf16[5,64,2048]{2,1,0:T(8,128)(2,1)S(1)}, u32[]{:S(2)}, u32[]{:S(2)}) collective-permute-start(bf16[5,64,2048]{2,1,0:T(8,128)(2,1)S(1)} %get-tuple-element.55), channel_id=1, source_target_pairs={{0,2},{1,3},{2,4},{3,5},{4,6},{5,7},{6,8},{7,9},{8,10},{9,11},{10,... | collective-permute-start | bytes 3932168 | tf_op jit(solution)/shard_map/ppermute | solution.py:23
  44.9 28.3 %collective-permute-start.5 = (bf16[5,64,2048]{2,1,0:T(8,128)(2,1)S(1)}, bf16[5,64,2048]{2,1,0:T(8,128)(2,1)S(1)}, u32[]{:S(2)}, u32[]{:S(2)}) collective-permute-start(bf16[5,64,2048]{2,1,0:T(8,128)(2,1)S(1)} %get-tuple-element.57), channel_id=1, source_target_pairs={{0,4},{1,1},{2,2},{3,3},{4,8},{5,5},{6,6},{7,7},{8,12},{9,9},{10,1... | collective-permute-start | bytes 3932168 | tf_op jit(solution)/shard_map/ppermute | solution.py:23
  46.8 26.4 %collective-permute-start.6 = (bf16[1,64,2048]{2,1,0:T(8,128)(2,1)S(1)}, bf16[1,64,2048]{2,1,0:T(8,128)(2,1)S(1)}, u32[]{:S(2)}, u32[]{:S(2)}) collective-permute-start(bf16[1,64,2048]{2,1,0:T(8,128)(2,1)S(1)} %get-tuple-element.58), channel_id=1, source_target_pairs={{0,4},{1,1},{2,2},{3,3},{4,8},{5,5},{6,6},{7,7},{8,12},{9,9},{10,1... | collective-permute-start | bytes 786440 | tf_op jit(solution)/shard_map/ppermute | solution.py:23
  49.9 28.9 %collective-permute-start.7 = (bf16[1,64,2048]{2,1,0:T(8,128)(2,1)S(1)}, bf16[1,64,2048]{2,1,0:T(8,128)(2,1)S(1)}, u32[]{:S(2)}, u32[]{:S(2)}) collective-permute-start(bf16[1,64,2048]{2,1,0:T(8,128)(2,1)S(1)} %get-tuple-element.60), channel_id=1, source_target_pairs={{0,2},{1,3},{2,4},{3,5},{4,6},{5,7},{6,8},{7,9},{8,10},{9,11},{10,... | collective-permute-start | bytes 786440 | tf_op jit(solution)/shard_map/ppermute | solution.py:23
  49.9 28.8 %collective-permute-start.8 = (bf16[8,1024]{1,0:T(8,128)(2,1)S(1)}, bf16[8,1024]{1,0:T(8,128)(2,1)S(1)}, u32[]{:S(2)}, u32[]{:S(2)}) collective-permute-start(bf16[8,1024]{1,0:T(8,128)(2,1)S(1)} %get-tuple-element.61), channel_id=1, source_target_pairs={{0,1},{1,2},{2,3},{3,4},{4,5},{5,6},{6,7},{7,8},{8,9},{9,10},{10,1... | collective-permute-start | bytes 49160 | tf_op jit(solution)/shard_map/ppermute | solution.py:23

commit v7 on v6

--- a/solution.py
+++ b/solution.py
@@ -16,7 +16,7 @@
 SMALL = pl.CostEstimate(flops=0, bytes_accessed=0, transcendentals=0)
 LITTLE = 1 << 20
 LINES = 8
-PIECES = 2
+PIECES = 4
 
 
 def send(value, pairs):

time: 79.8 us -> 79.7 us (level)
  no operation moved by 1% of the time
where the time goes in v7:
time: 79.7 us; the launch traced here: 79.4 us
  waiting for transfers between devices  44 us (55%)
  Pallas kernels  22.6 us (28%)
  starting transfers between devices  12.1 us (15%)
    ppermute x9, waiting for transfers between devices, send(): return lax.ppermute(value, 'inst', pairs)  44 us
    pallas_call x1, Pallas kernels, attend(): pl.pallas_call(attend_kernel, out_shape=shapes, in_specs=[pl.BlockSpec(me...  14 us
    ppermute x9, starting transfers between devices, send(): return lax.ppermute(value, 'inst', pairs)  12.1 us
    pallas_call x2, Pallas kernels, pack(): pl.pallas_call(functools.partial(pack_kernel, cuts), out_shape=shapes, in...  4.69 us
    pallas_call x3, Pallas kernels, place(): pl.pallas_call(functools.partial(place_kernel, rows, len(guests)), out_sh...  3.49 us
  transfers between devices with their start and end apart: 9, of which 4 were waited for; matrix products, arithmetic and copies ran while one was open for 0% of the time, Pallas kernels for 24%

profile of v7, /device:TPU:0, one launch (start us, length us, event | category | flops | bytes accessed | tf_op | source)
XLA Modules:
  0.0 79.4 jit_solution(9656751932440795123)
XLA Ops:
  0.6 2.6 %pack.2 = (bf16[12,32,2048]{2,1,0:T(8,128)(2,1)S(1)}, bf16[12,32,2048]{2,1,0:T(8,128)(2,1)S(1)}) custom-call(s32[4]{0:T(128)} %moves_ref.5, s32[4,3]{1,0:T(4,128)} %table_ref.3, bf16[48,32,2048]{2,1,0:T(8,128)(2,1)} %bitcast.2), custom_call_target="tpu_custom_call" | custom-call | tf_op jit(solution)/shard_map/pack/pallas_call | solution.py:62
  3.2 2.4 %collective-permute-start.3 = (bf16[12,32,2048]{2,1,0:T(8,128)(2,1)S(1)}, bf16[12,32,2048]{2,1,0:T(8,128)(2,1)S(1)}, u32[]{:S(2)}, u32[]{:S(2)}) collective-permute-start(bf16[12,32,2048]{2,1,0:T(8,128)(2,1)S(1)} %get-tuple-element.52), channel_id=1, source_target_pairs={{0,3},{1,4},{2,5},{3,6},{4,7},{5,8},{6,9},{7,10},{8,11},{9,12},{10... | collective-permute-start | bytes 4718600 | tf_op jit(solution)/shard_map/ppermute | solution.py:23
  5.7 0.8 collective-permute-start
  6.4 2.1 %pack.3 = (bf16[11,32,2048]{2,1,0:T(8,128)(2,1)S(1)}, bf16[1,32,2048]{2,1,0:T(8,128)(2,1)S(1)}) custom-call(s32[4]{0:T(128)} %moves_ref.5, s32[4,3]{1,0:T(4,128)} %table_ref.3, bf16[48,32,2048]{2,1,0:T(8,128)(2,1)} %bitcast.3), custom_call_target="tpu_custom_call" | custom-call | tf_op jit(solution)/shard_map/pack/pallas_call | solution.py:62
  8.5 14.0 %attend.1 = (bf16[2,4,8192]{2,1,0:T(4,128)(2,1)}, bf16[8,1024]{1,0:T(8,128)(2,1)S(1)}, bf16[8,1024]{1,0:T(8,128)(2,1)S(1)}, bf16[8,1024]{1,0:T(8,128)(2,1)S(1)}) custom-call(s32[4]{0:T(128)} %moves_ref.5, s32[4,3]{1,0:T(4,128)} %table_ref.3, s32[4]{0:T(128)} %lengths_ref.1, bf16[12,128,2048]{2,1,0:T(8,128)(2,1)} %pool_ref.1, bf16[2,4,8192]{2,1,0:T(4,128)(2,1)} %query_ref, ...), custom_call_target="tpu_custom_call" | custom-call | tf_op jit(solution)/shard_map/attend/pallas_call | solution.py:216
  22.5 1.5 %collective-permute-start.1 = (bf16[8,1024]{1,0:T(8,128)(2,1)S(1)}, bf16[8,1024]{1,0:T(8,128)(2,1)S(1)}, u32[]{:S(2)}, u32[]{:S(2)}) collective-permute-start(bf16[8,1024]{1,0:T(8,128)(2,1)S(1)} %get-tuple-element.49), channel_id=1, source_target_pairs={{0,2},{1,3},{2,4},{3,5},{4,6},{5,7},{6,8},{7,9},{8,10},{9,11},{10,... | collective-permute-start | bytes 49160 | tf_op jit(solution)/shard_map/ppermute | solution.py:23
  24.1 1.8 %collective-permute-start.2 = (bf16[8,1024]{1,0:T(8,128)(2,1)S(1)}, bf16[8,1024]{1,0:T(8,128)(2,1)S(1)}, u32[]{:S(2)}, u32[]{:S(2)}) collective-permute-start(bf16[8,1024]{1,0:T(8,128)(2,1)S(1)} %get-tuple-element.50), channel_id=1, source_target_pairs={{0,3},{1,4},{2,5},{3,6},{4,7},{5,8},{6,9},{7,10},{8,11},{9,12},{10... | collective-permute-start | bytes 49160 | tf_op jit(solution)/shard_map/ppermute | solution.py:23
  25.9 0.6 collective-permute-start.4
  26.4 13.0 %collective-permute-done.3.refs_0_ = bf16[12,32,2048]{2,1,0:T(8,128)(2,1)S(1)} collective-permute-done((bf16[12,32,2048]{2,1,0:T(8,128)(2,1)S(1)}, bf16[12,32,2048]{2,1,0:T(8,128)(2,1)S(1)}, u32[]{:S(2)}, u32[]{:S(2)}) %collective-permute-start.3) | collective-permute-done | bytes 1572896 | tf_op jit(solution)/shard_map/ppermute | solution.py:23
  39.5 1.1 %place.3.refs_3_ = bf16[36,32,2048]{2,1,0:T(8,128)(2,1)} custom-call(bf16[12,32,2048]{2,1,0:T(8,128)(2,1)S(1)} %collective-permute-done.3.refs_0_), custom_call_target="tpu_custom_call" | custom-call | tf_op jit(solution)/shard_map/place/pallas_call | solution.py:115
  40.6 4.2 %collective-permute-done.1.refs_2_ = bf16[8,1024]{1,0:T(8,128)(2,1)S(1)} collective-permute-done((bf16[8,1024]{1,0:T(8,128)(2,1)S(1)}, bf16[8,1024]{1,0:T(8,128)(2,1)S(1)}, u32[]{:S(2)}, u32[]{:S(2)}) %collective-permute-start.1) | collective-permute-done | bytes 16416 | tf_op jit(solution)/shard_map/ppermute | solution.py:23
  44.8 0.0 collective-permute-done.2.refs_3_
  44.9 0.0 collective-permute-done.whole_ref
  44.9 0.4 split.1
  45.3 1.9 %collective-permute-start.5 = (bf16[11,32,2048]{2,1,0:T(8,128)(2,1)S(1)}, bf16[11,32,2048]{2,1,0:T(8,128)(2,1)S(1)}, u32[]{:S(2)}, u32[]{:S(2)}) collective-permute-start(bf16[11,32,2048]{2,1,0:T(8,128)(2,1)S(1)} %get-tuple-element.57), channel_id=1, source_target_pairs={{0,4},{1,1},{2,2},{3,3},{4,8},{5,5},{6,6},{7,7},{8,12},{9,9},{10,1... | collective-permute-start | bytes 4325384 | tf_op jit(solution)/shard_map/ppermute | solution.py:23
  47.2 3.0 %collective-permute-start.6 = (bf16[1,32,2048]{2,1,0:T(8,128)(2,1)S(1)}, bf16[1,32,2048]{2,1,0:T(8,128)(2,1)S(1)}, u32[]{:S(2)}, u32[]{:S(2)}) collective-permute-start(bf16[1,32,2048]{2,1,0:T(8,128)(2,1)S(1)} %get-tuple-element.58), channel_id=1, source_target_pairs={{0,4},{1,1},{2,2},{3,3},{4,8},{5,5},{6,6},{7,7},{8,12},{9,9},{10,1... | collective-permute-start | bytes 393224 | tf_op jit(solution)/shard_map/ppermute | solution.py:23
  50.2 0.1 collective-permute-start.7
  50.3 0.1 collective-permute-start.8
  50.3 25.8 %collective-permute-done.4.refs_0_ = bf16[11,32,2048]{2,1,0:T(8,128)(2,1)S(1)} collective-permute-done((bf16[11,32,2048]{2,1,0:T(8,128)(2,1)S(1)}, bf16[11,32,2048]{2,1,0:T(8,128)(2,1)S(1)}, u32[]{:S(2)}, u32[]{:S(2)}) %collective-permute-start.4) | collective-permute-done | bytes 1441824 | tf_op jit(solution)/shard_map/ppermute | solution.py:23
  76.1 0.0 collective-permute-done.6.refs_2_
  76.1 0.0 collective-permute-done.5.refs_1_
  76.1 1.6 %place.4.refs_4_ = bf16[36,32,2048]{2,1,0:T(8,128)(2,1)} custom-call(bf16[11,32,2048]{2,1,0:T(8,128)(2,1)S(1)} %collective-permute-done.4.refs_0_, bf16[11,32,2048]{2,1,0:T(8,128)(2,1)S(1)} %collective-permute-done.5.refs_1_, bf16[1,32,2048]{2,1,0:T(8,128)(2,1)S(1)} %collective-permute-done.6.refs_2_, ...), custom_call_target="tpu_custom_call", output_to_operand_aliasing={{}: (3, {})} | custom-call | tf_op jit(solution)/shard_map/place/pallas_call | solution.py:115
  77.7 1.0 %collective-permute-done.7.refs_0_ = bf16[1,32,2048]{2,1,0:T(8,128)(2,1)S(1)} collective-permute-done((bf16[1,32,2048]{2,1,0:T(8,128)(2,1)S(1)}, bf16[1,32,2048]{2,1,0:T(8,128)(2,1)S(1)}, u32[]{:S(2)}, u32[]{:S(2)}) %collective-permute-start.7) | collective-permute-done | bytes 131104 | tf_op jit(solution)/shard_map/ppermute | solution.py:23
  78.7 0.0 collective-permute-done.8.refs_1_
  78.7 0.7 place.5
Async XLA Ops:
  3.2 36.2 %collective-permute-start.3 = (bf16[12,32,2048]{2,1,0:T(8,128)(2,1)S(1)}, bf16[12,32,2048]{2,1,0:T(8,128)(2,1)S(1)}, u32[]{:S(2)}, u32[]{:S(2)}) collective-permute-start(bf16[12,32,2048]{2,1,0:T(8,128)(2,1)S(1)} %get-tuple-element.52), channel_id=1, source_target_pairs={{0,3},{1,4},{2,5},{3,6},{4,7},{5,8},{6,9},{7,10},{8,11},{9,12},{10... | collective-permute-start | bytes 4718600 | tf_op jit(solution)/shard_map/ppermute | solution.py:23
  5.7 39.2 %collective-permute-start = (bf16[12,32,2048]{2,1,0:T(8,128)(2,1)S(1)}, bf16[12,32,2048]{2,1,0:T(8,128)(2,1)S(1)}, u32[]{:S(2)}, u32[]{:S(2)}) collective-permute-start(bf16[12,32,2048]{2,1,0:T(8,128)(2,1)S(1)} %get-tuple-element.48), channel_id=1, source_target_pairs={{0,1},{1,2},{2,3},{3,0},{4,5},{5,6},{6,7},{7,4},{8,9},{9,10},{10,1... | collective-permute-start | bytes 4718600 | tf_op jit(solution)/shard_map/ppermute | solution.py:23
  22.5 22.3 %collective-permute-start.1 = (bf16[8,1024]{1,0:T(8,128)(2,1)S(1)}, bf16[8,1024]{1,0:T(8,128)(2,1)S(1)}, u32[]{:S(2)}, u32[]{:S(2)}) collective-permute-start(bf16[8,1024]{1,0:T(8,128)(2,1)S(1)} %get-tuple-element.49), channel_id=1, source_target_pairs={{0,2},{1,3},{2,4},{3,5},{4,6},{5,7},{6,8},{7,9},{8,10},{9,11},{10,... | collective-permute-start | bytes 49160 | tf_op jit(solution)/shard_map/ppermute | solution.py:23
  24.1 20.8 %collective-permute-start.2 = (bf16[8,1024]{1,0:T(8,128)(2,1)S(1)}, bf16[8,1024]{1,0:T(8,128)(2,1)S(1)}, u32[]{:S(2)}, u32[]{:S(2)}) collective-permute-start(bf16[8,1024]{1,0:T(8,128)(2,1)S(1)} %get-tuple-element.50), channel_id=1, source_target_pairs={{0,3},{1,4},{2,5},{3,6},{4,7},{5,8},{6,9},{7,10},{8,11},{9,12},{10... | collective-permute-start | bytes 49160 | tf_op jit(solution)/shard_map/ppermute | solution.py:23
  25.9 50.2 %collective-permute-start.4 = (bf16[11,32,2048]{2,1,0:T(8,128)(2,1)S(1)}, bf16[11,32,2048]{2,1,0:T(8,128)(2,1)S(1)}, u32[]{:S(2)}, u32[]{:S(2)}) collective-permute-start(bf16[11,32,2048]{2,1,0:T(8,128)(2,1)S(1)} %get-tuple-element.55), channel_id=1, source_target_pairs={{0,2},{1,3},{2,4},{3,5},{4,6},{5,7},{6,8},{7,9},{8,10},{9,11},{10,... | collective-permute-start | bytes 4325384 | tf_op jit(solution)/shard_map/ppermute | solution.py:23
  45.3 30.8 %collective-permute-start.5 = (bf16[11,32,2048]{2,1,0:T(8,128)(2,1)S(1)}, bf16[11,32,2048]{2,1,0:T(8,128)(2,1)S(1)}, u32[]{:S(2)}, u32[]{:S(2)}) collective-permute-start(bf16[11,32,2048]{2,1,0:T(8,128)(2,1)S(1)} %get-tuple-element.57), channel_id=1, source_target_pairs={{0,4},{1,1},{2,2},{3,3},{4,8},{5,5},{6,6},{7,7},{8,12},{9,9},{10,1... | collective-permute-start | bytes 4325384 | tf_op jit(solution)/shard_map/ppermute | solution.py:23
  47.2 28.9 %collective-permute-start.6 = (bf16[1,32,2048]{2,1,0:T(8,128)(2,1)S(1)}, bf16[1,32,2048]{2,1,0:T(8,128)(2,1)S(1)}, u32[]{:S(2)}, u32[]{:S(2)}) collective-permute-start(bf16[1,32,2048]{2,1,0:T(8,128)(2,1)S(1)} %get-tuple-element.58), channel_id=1, source_target_pairs={{0,4},{1,1},{2,2},{3,3},{4,8},{5,5},{6,6},{7,7},{8,12},{9,9},{10,1... | collective-permute-start | bytes 393224 | tf_op jit(solution)/shard_map/ppermute | solution.py:23
  50.2 28.5 %collective-permute-start.7 = (bf16[1,32,2048]{2,1,0:T(8,128)(2,1)S(1)}, bf16[1,32,2048]{2,1,0:T(8,128)(2,1)S(1)}, u32[]{:S(2)}, u32[]{:S(2)}) collective-permute-start(bf16[1,32,2048]{2,1,0:T(8,128)(2,1)S(1)} %get-tuple-element.60), channel_id=1, source_target_pairs={{0,2},{1,3},{2,4},{3,5},{4,6},{5,7},{6,8},{7,9},{8,10},{9,11},{10,... | collective-permute-start | bytes 393224 | tf_op jit(solution)/shard_map/ppermute | solution.py:23
  50.3 28.5 %collective-permute-start.8 = (bf16[8,1024]{1,0:T(8,128)(2,1)S(1)}, bf16[8,1024]{1,0:T(8,128)(2,1)S(1)}, u32[]{:S(2)}, u32[]{:S(2)}) collective-permute-start(bf16[8,1024]{1,0:T(8,128)(2,1)S(1)} %get-tuple-element.61), channel_id=1, source_target_pairs={{0,1},{1,2},{2,3},{3,4},{4,5},{5,6},{6,7},{7,8},{8,9},{9,10},{10,1... | collective-permute-start | bytes 49160 | tf_op jit(solution)/shard_map/ppermute | solution.py:23
